TPU v7x, 32 devices: a whole 2x2x4 slice. The times are simulated.
32 devices in a mesh: grp: 2 (over y), lat: 4 (over z), lon: 2 (over x), role: 2 (over core).
Axes of the slice: x: 2, y: 2, z: 4, core: 2. Of those that a mesh axis runs over, the one named last changes fastest.
Arguments:
- eastern_edge_current: float32 [8, 128, 256], P('lon', ('grp', 'lat', 'role')), parts along dimension 1, may hold values from -1.5 to 1.5
- northern_edge_current: float32 [8, 128, 256], P('lon', ('grp', 'lat', 'role')), parts along dimension 1, may hold values from -1.5 to 1.5
- thermal_anomaly: float32 [8, 128, 256], P('lon', ('grp', 'lat', 'role')), parts along dimension 1, may hold values from -6 to 6
- prior_warming: float32 [8, 128, 256], P('lon', ('grp', 'lat', 'role')), parts along dimension 1, may hold values from 0 to 0.5
- solute_fields: float32 [24, 8, 128, 256], P(None, None, ('grp', 'lat', 'role'), 'lon'), parts along dimension 2, may hold values from -6 to 6
- submerged_layer_count: int32 [128, 256], P(('grp', 'lat', 'role')), parts along dimension 0, may hold values from 0 to 8
- reaction_rates: float32 [24, 24], replicated, may hold values from -1.25 to 1.25
Outputs:
- u_out: float32 [8, 128, 256], P('lon', ('grp', 'lat', 'role')), parts along dimension 1
- v_out: float32 [8, 128, 256], P('lon', ('grp', 'lat', 'role')), parts along dimension 1
- temp_out: float32 [8, 128, 256], P('lon', ('grp', 'lat', 'role')), parts along dimension 1
- heating_out: float32 [8, 128, 256], P('lon', ('grp', 'lat', 'role')), parts along dimension 1
- tracers_out: float32 [24, 8, 128, 256], P(None, None, ('grp', 'lat', 'role'), 'lon'), parts along dimension 2
There are 2 independent parts, one for each index of `grp`. A program takes and returns all parts, laid end to end along the dimension named above; an argument that names none is the same for every part. Nothing has to cross between parts.
All inputs are finite; a program needn't handle non-finite values.
Results may differ from a plain program's by a relative error of at most 0.0001.
Values sent between devices are 32-bit elements; how exact they have to be, the bound alone decides.
A program may use at most 64 MiB of HBM per device.

v0:
```python
import functools

import jax
import jax.numpy as jnp
from jax import lax
from jax.experimental import pallas as pl
from jax.experimental.pallas import tpu as pltpu
from jax.sharding import PartitionSpec as P

ROWS = 8
LANES = 128
PAD = 4
EXT = ROWS + 2 * PAD
PAIR = 2
VMEM = 40 * 1024 * 1024
F32 = jnp.float32


def east(q):
    lane = lax.broadcasted_iota(jnp.int32, q.shape, q.ndim - 1)
    return jnp.where(lane < q.shape[-1] - 1, pltpu.roll(q, q.shape[-1] - 1, q.ndim - 1), 0.0)


def west(q):
    lane = lax.broadcasted_iota(jnp.int32, q.shape, q.ndim - 1)
    return jnp.where(lane > 0, pltpu.roll(q, 1, q.ndim - 1), 0.0)


def north(q):
    return pltpu.roll(q, q.shape[-2] - 1, q.ndim - 2)


def south(q):
    return pltpu.roll(q, 1, q.ndim - 2)


def lap(q):
    return east(q) + west(q) + north(q) + south(q) - 4.0 * q


def kernel(
    sizes,
    u_hbm, v_hbm, t_hbm, h_hbm, c_hbm, n_hbm, r_hbm,
    u_out, v_out, t_out, h_out, c_out,
    pk_n, pk_s, rc_n, rc_s, cnt_n, cnt_s, ext, ext_n, t_base, wet_strip,
    c_mid, row_lo, row_hi, col_ed, got_n, got_s, got_w, got_e,
    f_send, f_recv, h_send, h_recv,
    u_in, v_in, t_in, h_in, c_in, n_in, r_in, in_sem,
    d_ssem, d_rsem, c0_ssem, c0_rsem, c1_ssem, c1_rsem, f_ssem, f_rsem, h_ssem, h_rsem,
):
    tracers, depth, share, nlon, nrole, nstrip = sizes
    width = nlon * LANES
    arrays = (
        (u_hbm, u_in), (v_hbm, v_in), (t_hbm, t_in), (h_hbm, h_in), (n_hbm, n_in), (c_hbm, c_in), (r_hbm, r_in),
    )
    loads = [pltpu.make_async_copy(a, b, in_sem.at[i]) for i, (a, b) in enumerate(arrays)]
    for load in loads:
        load.start()
    s = lax.axis_index("lat") * nrole + lax.axis_index("role")
    col = lax.axis_index("lon")
    has_n, has_s = s < nstrip - 1, s > 0
    has_e, has_w = col < nlon - 1, col > 0
    sn, ss = lax.rem(s + 1, nstrip), lax.rem(s + nstrip - 1, nstrip)
    dev_n = {"lat": sn // nrole, "role": lax.rem(sn, nrole)}
    dev_s = {"lat": ss // nrole, "role": lax.rem(ss, nrole)}
    dev_e = {"lon": lax.rem(col + 1, nlon)}
    dev_w = {"lon": lax.rem(col + nlon - 1, nlon)}

    barrier = pltpu.get_barrier_semaphore()

    def greet(dev):
        pl.semaphore_signal(barrier, inc=1, device_id=dev, device_id_type=pl.DeviceIdType.MESH)

    pl.when(has_n)(lambda: greet(dev_n))
    pl.when(has_s)(lambda: greet(dev_s))
    for d in range(1, nlon):
        greet({"lon": lax.rem(col + d, nlon)})

    def copy(src, dst, ssem, rsem, dev):
        return pltpu.make_async_remote_copy(
            src_ref=src, dst_ref=dst, send_sem=ssem, recv_sem=rsem,
            device_id=dev, device_id_type=pl.DeviceIdType.MESH,
        )

    def start(copies):
        for c, send, _ in copies:
            pl.when(send)(c.start)

    def wait_recv(copies):
        for c, _, recv in copies:
            pl.when(recv)(c.wait_recv)

    def wait_send(copies):
        for c, send, _ in copies:
            pl.when(send)(c.wait_send)

    for load in loads[:5]:
        load.wait()
    pk_n[:, 0:3, :] = v_in[:, 5:8, :]
    pk_n[:, 3:5, :] = u_in[:, 6:8, :]
    pk_n[:, 5:7, :] = t_in[:, 6:8, :]
    pk_n[:, 7:8, :] = h_in[:, 7:8, :]
    pk_s[:, 0:2, :] = u_in[:, 0:2, :]
    pk_s[:, 2:4, :] = v_in[:, 0:2, :]
    pk_s[:, 4:6, :] = t_in[:, 0:2, :]
    pk_s[:, 6:7, :] = h_in[:, 0:1, :]
    pk_s[:, 7:8, :] = h_in[:, 0:1, :]

    lane = lax.broadcasted_iota(jnp.int32, (ROWS, LANES), 1)
    row = lax.broadcasted_iota(jnp.int32, (ROWS, LANES), 0)

    def pack(m, k, x):
        row_lo[m, k] = x[:, 0, :]
        row_hi[m, k] = x[:, ROWS - 1, :]
        acc = x[0]
        for t in range(1, tracers):
            here = (lane == 2 * t - 1) | (lane == 2 * t)
            acc = jnp.where(here, pltpu.roll(x[t], 2 * t, 1), acc)
        col_ed[m, k] = acc

    dyn = [
        (copy(pk_n, rc_s, d_ssem.at[0], d_rsem.at[0], dev_n), has_n, has_s),
        (copy(pk_s, rc_n, d_ssem.at[1], d_rsem.at[1], dev_s), has_s, has_n),
        (copy(n_in, cnt_s, d_ssem.at[2], d_rsem.at[2], dev_n), has_n, has_s),
        (copy(n_in, cnt_n, d_ssem.at[3], d_rsem.at[3], dev_s), has_s, has_n),
    ]
    first = [
        (copy(row_hi.at[0], got_s.at[0], c0_ssem.at[0], c0_rsem.at[0], dev_n), has_n, has_s),
        (copy(row_lo.at[0], got_n.at[0], c0_ssem.at[1], c0_rsem.at[1], dev_s), has_s, has_n),
        (copy(col_ed.at[0], got_w.at[0], c0_ssem.at[2], c0_rsem.at[2], dev_e), has_e, has_w),
        (copy(col_ed.at[0], got_e.at[0], c0_ssem.at[3], c0_rsem.at[3], dev_w), has_w, has_e),
    ]

    def second(g):
        two = pl.ds(g * PAIR, PAIR)
        routes = (
            (row_hi, got_s, dev_n, has_n, has_s), (row_lo, got_n, dev_s, has_s, has_n),
            (col_ed, got_w, dev_e, has_e, has_w), (col_ed, got_e, dev_w, has_w, has_e),
        )
        return [
            (copy(a.at[1, two], b.at[1, two], c1_ssem.at[i, g], c1_rsem.at[i, g], dev), send, recv)
            for i, (a, b, dev, send, recv) in enumerate(routes)
        ]

    def faces(m):
        out = []
        for d in range(1, nlon):
            p = lax.rem(col + d, nlon)
            out.append(copy(f_send.at[m, p], f_recv.at[m, col], f_ssem.at[m, d], f_rsem.at[m, d], {"lon": p}))
        return out

    def heats(m):
        out = []
        for d in range(1, nlon):
            p = lax.rem(col + d, nlon)
            out.append(copy(h_send.at[m, p], h_recv.at[m, col], h_ssem.at[m, d], h_rsem.at[m, d], {"lon": p}))
        return out

    pl.semaphore_wait(barrier, nlon - 1 + jnp.minimum(s, 1) + jnp.minimum(nstrip - 1 - s, 1))
    start(dyn)
    for load in loads[5:]:
        load.wait()
    for k in range(depth):
        pack(0, k, c_in[:, k])
    start(first)

    @pl.when(jnp.logical_not(has_s))
    def _():
        rc_s[...] = jnp.zeros_like(rc_s)
        cnt_s[...] = jnp.zeros_like(cnt_s)
        got_s[...] = jnp.zeros_like(got_s)

    @pl.when(jnp.logical_not(has_n))
    def _():
        rc_n[...] = jnp.zeros_like(rc_n)
        cnt_n[...] = jnp.zeros_like(cnt_n)
        got_n[...] = jnp.zeros_like(got_n)

    @pl.when(jnp.logical_not(has_w))
    def _():
        got_w[...] = jnp.zeros_like(got_w)

    @pl.when(jnp.logical_not(has_e))
    def _():
        got_e[...] = jnp.zeros_like(got_e)

    wide = tracers * ROWS
    spread = (
        lax.broadcasted_iota(jnp.int32, (wide, tracers), 0) // ROWS
        == lax.broadcasted_iota(jnp.int32, (wide, tracers), 1)
    ).astype(F32)
    gather = (
        lax.broadcasted_iota(jnp.int32, (tracers, wide), 1) // ROWS
        == lax.broadcasted_iota(jnp.int32, (tracers, wide), 0)
    ).astype(F32)
    exact = lax.Precision.HIGHEST
    rates = jnp.dot(
        spread, jnp.dot(r_in[...], gather, precision=exact, preferred_element_type=F32),
        precision=exact, preferred_element_type=F32,
    )
    same_row = (
        lax.broadcasted_iota(jnp.int32, (wide, wide), 0) % ROWS
        == lax.broadcasted_iota(jnp.int32, (wide, wide), 1) % ROWS
    )
    rates = jnp.where(same_row, rates, 0.0)
    rates_hi = rates.astype(jnp.bfloat16)
    rates_lo = (rates - rates_hi.astype(F32)).astype(jnp.bfloat16)

    zero = jnp.zeros((share, PAD, width), F32)
    for f in range(4):
        ext[f, :, 0:PAD, :] = zero
        ext[f, :, PAD + ROWS :, :] = zero
    ext_n[0:PAD, :] = jnp.zeros((PAD, width), jnp.int32)
    ext_n[PAD + ROWS :, :] = jnp.zeros((PAD, width), jnp.int32)
    for f, ref in enumerate((u_in, v_in, t_in, h_in)):
        ext[f, :, PAD : PAD + ROWS, :] = ref[...]
    ext_n[PAD : PAD + ROWS, :] = n_in[...]

    wait_recv(dyn)
    ext[0, :, 2:4, :] = rc_s[:, 3:5, :]
    ext[1, :, 1:4, :] = rc_s[:, 0:3, :]
    ext[2, :, 2:4, :] = rc_s[:, 5:7, :]
    ext[3, :, 3:4, :] = rc_s[:, 7:8, :]
    ext[0, :, 12:14, :] = rc_n[:, 0:2, :]
    ext[1, :, 12:14, :] = rc_n[:, 2:4, :]
    ext[2, :, 12:14, :] = rc_n[:, 4:6, :]
    ext[3, :, 12:13, :] = rc_n[:, 6:7, :]
    ext_n[2:4, :] = cnt_s[6:8, :]
    ext_n[12:14, :] = cnt_n[0:2, :]

    shape = (share, EXT, width)
    level = col * share + lax.broadcasted_iota(jnp.int32, shape, 0)
    wet = (level < ext_n[...][None]).astype(F32)
    wet_u = wet * east(wet)
    wet_v = wet * north(wet)
    spot = (s * ROWS - PAD + lax.broadcasted_iota(jnp.int32, shape, 1)).astype(F32)
    fcor = 0.3 * (2.0 * (spot + 0.5) / (nstrip * ROWS) - 1.0)

    def advance(u, v, t):
        new_u = wet_u * (u + 0.1 * lap(u) + fcor * v - 0.2 * (east(t) - t))
        new_v = wet_v * (v + 0.1 * lap(v) - fcor * u - 0.2 * (north(t) - t))
        return new_u, new_v

    def publish(m, u, v):
        for p in range(nlon):
            lo = p * LANES
            cols = slice(lo, lo + LANES)
            v_edge = jnp.zeros((ROWS, LANES), F32)
            u_edge = jnp.zeros((ROWS, LANES), F32)
            for l in range(share):
                f_send[m, p, l] = u[l, PAD : PAD + ROWS, cols]
                f_send[m, p, share + l] = v[l, PAD : PAD + ROWS, cols]
                v_edge = jnp.where(row == l, v[l, PAD - 1 : PAD, cols], v_edge)
                if p:
                    u_edge = jnp.where(lane == l, u[l, PAD : PAD + ROWS, lo - 1 : lo], u_edge)
            f_send[m, p, 2 * share] = v_edge
            f_send[m, p, 2 * share + 1] = u_edge
        for c in faces(m):
            c.start()
        f_recv[m, col] = f_send[m, col]

    u0, v0, t0 = ext[0], ext[1], ext[2]
    u1, v1 = advance(u0, v0, t0)
    publish(0, u1, v1)
    t1 = wet * (t0 + 0.1 * lap(t0) + 0.5 * ext[3])
    u2, v2 = advance(u1, v1, t1)
    publish(1, u2, v2)
    u_out[...] = u2[:, PAD : PAD + ROWS, :]
    v_out[...] = v2[:, PAD : PAD + ROWS, :]
    t_base[...] = (wet * (t1 + 0.1 * lap(t1)))[:, PAD : PAD + ROWS, :]
    wet_strip[...] = wet[:, PAD : PAD + ROWS, :]

    depth_here = n_in[:, pl.ds(pl.multiple_of(col * LANES, LANES), LANES)]

    def tile_step(m, source, target):
        coefs, sides, light = {}, {}, {}
        state = [jnp.zeros((ROWS, LANES), F32), jnp.ones((ROWS, LANES), F32)]

        def prepare(k):
            p, l = k // share, k % share
            u = f_recv[m, p, l]
            v = f_recv[m, p, share + l]
            v_s = jnp.where(row == 0, f_recv[m, p, 2 * share, l : l + 1, :], pltpu.roll(v, 1, 0))
            u_w = jnp.where(lane == 0, f_recv[m, p, 2 * share + 1, :, l : l + 1], pltpu.roll(u, 1, 1))
            a_0 = 1.0 - 0.5 * (
                (jnp.maximum(u, 0.0) - jnp.minimum(u_w, 0.0)) + (jnp.maximum(v, 0.0) - jnp.minimum(v_s, 0.0))
            )
            coefs[k] = (
                a_0, -0.5 * jnp.minimum(u, 0.0), 0.5 * jnp.maximum(u_w, 0.0),
                -0.5 * jnp.minimum(v, 0.0), 0.5 * jnp.maximum(v_s, 0.0),
            )
            sides[k] = jnp.where(
                lane % 2 == 0, pltpu.roll(got_w[m, k], 1, 1), pltpu.roll(got_e[m, k], LANES - 1, 1)
            )

        def advect(k, t):
            a_0, a_e, a_w, a_n, a_s = coefs[k]
            x = source[t, k]
            edge = pltpu.roll(sides[k], (LANES - 2 * t) % LANES, 1)
            x_n = jnp.where(row == ROWS - 1, got_n[m, k, t : t + 1, :], pltpu.roll(x, ROWS - 1, 0))
            x_s = jnp.where(row == 0, got_s[m, k, t : t + 1, :], pltpu.roll(x, 1, 0))
            x_e = jnp.where(lane == LANES - 1, edge, pltpu.roll(x, LANES - 1, 1))
            x_w = jnp.where(lane == 0, edge, pltpu.roll(x, 1, 1))
            return a_0 * x + (a_e * x_e + a_w * x_w) + (a_n * x_n + a_s * x_s)

        def shine(k):
            p, l = k // share, k % share
            prepare(k)
            lead = advect(k, 0)
            wet_k = (k < depth_here).astype(F32)
            tau, top = state
            tau = tau + (0.1 + 0.3 * jnp.maximum(lead, 0.0))
            below = jnp.exp(-tau)
            h_send[m, p, l] = 2.0 * wet_k * (top - below)
            light[k] = (lead, wet_k, top)
            state[:] = [tau, below]
            if k == depth - 1:
                for c in heats(m):
                    c.start()
                h_recv[m, col] = h_send[m, col]

        groups = depth // PAIR
        held = {}
        for g in range(groups + 1):
            if g < groups:
                if m:
                    wait_recv(second(g))
                levels = range(g * PAIR, (g + 1) * PAIR)
                for k in levels:
                    shine(k)
                adv = [
                    jnp.concatenate([light[k][0]] + [advect(k, t) for t in range(1, tracers)], axis=0)
                    for k in levels
                ]
                hi = [a.astype(jnp.bfloat16) for a in adv]
                lo = [(a - b.astype(F32)).astype(jnp.bfloat16) for a, b in zip(adv, hi)]
                held[g] = (adv, jnp.concatenate(hi, axis=1), jnp.concatenate(lo, axis=1))
            if g > 0:
                adv, hi, lo = held.pop(g - 1)
                r = (
                    jnp.dot(rates_hi, hi, preferred_element_type=F32)
                    + jnp.dot(rates_hi, lo, preferred_element_type=F32)
                    + jnp.dot(rates_lo, hi, preferred_element_type=F32)
                )
                for n in range(PAIR):
                    k = (g - 1) * PAIR + n
                    _, wet_k, top = light[k]
                    gain = r[:, n * LANES : (n + 1) * LANES].reshape(tracers, ROWS, LANES)
                    new = wet_k * (adv[n].reshape(tracers, ROWS, LANES) + (0.5 * top) * gain)
                    target[:, k] = new
                    if m == 0:
                        pack(1, k, new)
                if m == 0:
                    start(second(g - 1))

    wait_recv(first)
    for c in faces(0):
        c.wait_recv()
    tile_step(0, c_in, c_mid)
    for c in faces(1):
        c.wait_recv()
    tile_step(1, c_mid, c_out)

    for c in heats(0):
        c.wait_recv()
    for p in range(nlon):
        cols = slice(p * LANES, (p + 1) * LANES)
        t_out[:, :, cols] = t_base[:, :, cols] + 0.5 * wet_strip[:, :, cols] * h_recv[0, p]
    wait_send(dyn)
    wait_send(first)
    for g in range(depth // PAIR):
        wait_send(second(g))
    for m in range(2):
        for c in faces(m):
            c.wait_send()
        for c in heats(m):
            c.wait_send()
    for c in heats(1):
        c.wait_recv()
    for p in range(nlon):
        h_out[:, :, p * LANES : (p + 1) * LANES] = h_recv[1, p]


def store(*refs):
    sources, results, sem = refs[:5], refs[5:10], refs[10]
    saves = [pltpu.make_async_copy(a, b, sem.at[i]) for i, (a, b) in enumerate(zip(sources, results))]
    for save in saves:
        save.start()
    for save in saves:
        save.wait()


def shards(sizes, u, v, t, h, c, n, r):
    tracers, depth, share, nlon, _, _ = sizes
    strip = jax.ShapeDtypeStruct(u.shape, F32)
    tile = (ROWS, LANES)
    strip_buf = pltpu.VMEM(u.shape, F32)
    dma = pltpu.SemaphoreType.DMA
    hbm = pl.BlockSpec(memory_space=pltpu.HBM)
    vmem = pl.BlockSpec(memory_space=pltpu.VMEM)
    outs = pl.pallas_call(
        functools.partial(kernel, sizes),
        out_shape=(strip_buf, strip_buf, strip_buf, strip_buf, pltpu.VMEM(c.shape, F32)),
        in_specs=[hbm] * 7,
        out_specs=(vmem,) * 5,
        scratch_shapes=[
            strip_buf, strip_buf, strip_buf, strip_buf,
            pltpu.VMEM(n.shape, jnp.int32), pltpu.VMEM(n.shape, jnp.int32),
            pltpu.VMEM((4, share, EXT, u.shape[2]), F32),
            pltpu.VMEM((EXT, u.shape[2]), jnp.int32),
            strip_buf, strip_buf,
            pltpu.VMEM(c.shape, F32),
            pltpu.VMEM((2, depth, tracers, LANES), F32),
            pltpu.VMEM((2, depth, tracers, LANES), F32),
            pltpu.VMEM((2, depth) + tile, F32),
            pltpu.VMEM((2, depth, tracers, LANES), F32),
            pltpu.VMEM((2, depth, tracers, LANES), F32),
            pltpu.VMEM((2, depth) + tile, F32),
            pltpu.VMEM((2, depth) + tile, F32),
            pltpu.VMEM((2, nlon, 2 * share + 2) + tile, F32),
            pltpu.VMEM((2, nlon, 2 * share + 2) + tile, F32),
            pltpu.VMEM((2, nlon, share) + tile, F32),
            pltpu.VMEM((2, nlon, share) + tile, F32),
            strip_buf, strip_buf, strip_buf, strip_buf, pltpu.VMEM(c.shape, F32),
            pltpu.VMEM(n.shape, jnp.int32), pltpu.VMEM(r.shape, F32), dma((7,)),
            dma((4,)), dma((4,)), dma((4,)), dma((4,)),
            dma((4, depth)), dma((4, depth)),
            dma((2, nlon)), dma((2, nlon)), dma((2, nlon)), dma((2, nlon)),
        ],
        compiler_params=pltpu.CompilerParams(
            collective_id=0, has_side_effects=True, vmem_limit_bytes=VMEM
        ),
    )(*(pltpu.with_memory_space_constraint(x, pltpu.HBM) for x in (u, v, t, h, c, n, r)))
    return pl.pallas_call(
        store,
        out_shape=(strip, strip, strip, strip, jax.ShapeDtypeStruct(c.shape, F32)),
        in_specs=[vmem] * 5,
        out_specs=(hbm,) * 5,
        scratch_shapes=[dma((5,))],
        compiler_params=pltpu.CompilerParams(vmem_limit_bytes=VMEM),
    )(*outs)


def solution(mesh):
    nlon, nrole = mesh.shape["lon"], mesh.shape["role"]
    nstrip = mesh.shape["lat"] * nrole
    strip = P("lon", ("grp", "lat", "role"), None)
    tile = P(None, None, ("grp", "lat", "role"), "lon")

    def run(u, v, t, h, c, n, r):
        sizes = (c.shape[0], c.shape[1], u.shape[0] // nlon, nlon, nrole, nstrip)
        return jax.shard_map(
            functools.partial(shards, sizes),
            mesh=mesh,
            in_specs=(strip, strip, strip, strip, tile, P(("grp", "lat", "role"), None), P()),
            out_specs=(strip, strip, strip, strip, tile),
            check_vma=False,
        )(u, v, t, h, c, n, r)

    return run
```

profile of v0, /device:TPU:0, one launch (start us, length us, event | category | flops | bytes accessed | tf_op | source)
XLA Modules:
  0.0 17.4 jit_solution(14560874609802148325)
XLA Ops:
  0.6 15.7 %shard_map.110 = (f32[4,8,256]{2,1,0:T(8,128)S(1)}, f32[4,8,256]{2,1,0:T(8,128)S(1)}, f32[4,8,256]{2,1,0:T(8,128)S(1)}, f32[4,8,256]{2,1,0:T(8,128)S(1)}, f32[24,8,8,128]{3,2,1,0:T(8,128)S(1)}) custom-call(f32[4,8,256]{2,1,0:T(8,128)} %u_hbm.1, f32[4,8,256]{2,1,0:T(8,128)} %v_hbm.1, f32[4,8,256]{2,1,0:T(8,128)} %t_hbm.1, f32[4,8,256]{2,1,0:T(8,128)} %h_hbm.1, ...), custom_call_target="tpu_custom_call" | custom-call | tf_op jit(solution)/shard_map/pallas_call | solution.py:401
  16.4 1.0 %shard_map.111 = (f32[4,8,256]{2,1,0:T(8,128)}, f32[4,8,256]{2,1,0:T(8,128)}, f32[4,8,256]{2,1,0:T(8,128)}, f32[4,8,256]{2,1,0:T(8,128)}, f32[24,8,8,128]{3,2,1,0:T(8,128)}) custom-call(f32[4,8,256]{2,1,0:T(8,128)S(1)} %get-tuple-element.10.refs_0_, f32[4,8,256]{2,1,0:T(8,128)S(1)} %get-tuple-element.11.refs_1_, f32[4,8,256]{2,1,0:T(8,128)S(1)} %get-tuple-element.12.refs_2_, ...), custom_call_target="tpu_custom_call" | custom-call | tf_op jit(solution)/shard_map/pallas_call | solution.py:434
where the time goes:
time: 17.5 us; the launch traced here: 17.4 us
  Pallas kernels  16.7 us (95%)
  between operations  0.64 us (4%)
    pallas_call x1, Pallas kernels, shards(): pl.pallas_call(functools.partial(kernel, sizes), out_shape=(strip_buf, st...  15.7 us
    pallas_call x1, Pallas kernels, shards(): pl.pallas_call(store, out_shape=(strip, strip, strip, strip, jax.ShapeDty...  0.97 us

commit v1 on v0

v1 whole, which is shorter than its diff:
```python
import functools

import jax
import jax.numpy as jnp
from jax import lax
from jax.experimental import pallas as pl
from jax.experimental.pallas import tpu as pltpu
from jax.sharding import PartitionSpec as P

ROWS = 8
LANES = 128
EXT = 2 * ROWS
WIDE = 2 * LANES
PAIR = 2
STEP = 4
GROUP = 8
VMEM = 40 * 1024 * 1024
F32 = jnp.float32
EXACT = lax.Precision.HIGHEST


def east(q):
    return pltpu.roll(q, q.shape[-1] - 1, q.ndim - 1)


def west(q):
    return pltpu.roll(q, 1, q.ndim - 1)


def north(q):
    return pltpu.roll(q, q.shape[-2] - 1, q.ndim - 2)


def south(q):
    return pltpu.roll(q, 1, q.ndim - 2)


def lap(q):
    return east(q) + west(q) + north(q) + south(q) - 4.0 * q


def upwind(u, u_w, v, v_s):
    u_neg, v_neg = jnp.minimum(u, 0.0), jnp.minimum(v, 0.0)
    uw_pos, vs_pos = jnp.maximum(u_w, 0.0), jnp.maximum(v_s, 0.0)
    a_0 = 1.0 - 0.5 * (
        (jnp.maximum(u, 0.0) - jnp.minimum(u_w, 0.0)) + (jnp.maximum(v, 0.0) - jnp.minimum(v_s, 0.0))
    )
    return a_0, -0.5 * u_neg, 0.5 * uw_pos, -0.5 * v_neg, 0.5 * vs_pos


def mix(a, x, x_e, x_w, x_n, x_s):
    return a[0] * x + (a[1] * x_e + a[2] * x_w) + (a[3] * x_n + a[4] * x_s)


def split(a):
    hi = a.astype(jnp.bfloat16)
    return hi, (a - hi.astype(F32)).astype(jnp.bfloat16)


def product(a, b):
    a_hi, a_lo = a
    b_hi, b_lo = b
    return (
        jnp.dot(a_hi, b_hi, preferred_element_type=F32)
        + jnp.dot(a_hi, b_lo, preferred_element_type=F32)
        + jnp.dot(a_lo, b_hi, preferred_element_type=F32)
    )


def kernel(
    sizes,
    u_hbm, v_hbm, t_hbm, h_hbm, c_hbm, n_hbm, r_hbm,
    out, c_out,
    strips, ext, edge_s, edge_x, cnt, c_in, c_mid, row_n, row_s, ring_n, ring_s,
    col_ed, got_e, got_w, cor, ring_c, cex, cec, cf1, t_base, o_send, r_in, in_sem,
    x_ss, x_rs, hx_ss, hx_rs, n_ss, n_rs, s_ss, s_rs, ex_ss, ex_rs, en_ss, en_rs, es_ss, es_rs,
    k_ss, k_rs, c_ss, c_rs, q_ss, q_rs, uv_ss, uv_rs, t_ss, t_rs, h_ss, h_rs,
):
    tracers, depth, share, nlon, nrole, nstrip = sizes
    loads = [pltpu.make_async_copy(a, strips.at[i], in_sem.at[i]) for i, a in enumerate((u_hbm, v_hbm, t_hbm, h_hbm))]
    loads.append(pltpu.make_async_copy(n_hbm, cnt.at[0:ROWS], in_sem.at[4]))
    loads.append(pltpu.make_async_copy(c_hbm, c_in, in_sem.at[5]))
    loads.append(pltpu.make_async_copy(r_hbm, r_in, in_sem.at[6]))
    for load in loads:
        load.start()

    s = lax.axis_index("lat") * nrole + lax.axis_index("role")
    col = lax.axis_index("lon")
    has_n, has_s = s < nstrip - 1, s > 0
    has_e, has_w = col < nlon - 1, col > 0
    sn, ss = lax.rem(s + 1, nstrip), lax.rem(s + nstrip - 1, nstrip)
    to_n = {"lat": sn // nrole, "role": lax.rem(sn, nrole)}
    to_s = {"lat": ss // nrole, "role": lax.rem(ss, nrole)}
    lon_e, lon_w = lax.rem(col + 1, nlon), lax.rem(col + nlon - 1, nlon)

    def others(first):
        return [(d, lax.rem(col + d, nlon)) for d in range(first, nlon)]

    barrier = pltpu.get_barrier_semaphore()

    def greet(dev):
        pl.semaphore_signal(barrier, inc=1, device_id=dev, device_id_type=pl.DeviceIdType.MESH)

    for d, p in others(1):
        greet({"lon": p})

    @pl.when(has_n)
    def _():
        for d, p in others(0):
            greet(dict(to_n, lon=p))

    @pl.when(has_s)
    def _():
        for d, p in others(0):
            greet(dict(to_s, lon=p))

    def copy(src, dst, ssem, rsem, dev):
        return pltpu.make_async_remote_copy(
            src_ref=src, dst_ref=dst, send_sem=ssem, recv_sem=rsem,
            device_id=dev, device_id_type=pl.DeviceIdType.MESH,
        )

    def start(cond, copies):
        if cond is None:
            for c in copies:
                c.start()
        else:
            pl.when(cond)(lambda: start(None, copies))

    def wait_recv(cond, copies):
        if cond is None:
            for c in copies:
                c.wait_recv()
        else:
            pl.when(cond)(lambda: wait_recv(None, copies))

    def wait_send(cond, copies):
        if cond is None:
            for c in copies:
                c.wait_send()
        else:
            pl.when(cond)(lambda: wait_send(None, copies))

    def cols(p):
        return pl.ds(pl.multiple_of(p * LANES, LANES), LANES)

    main = pl.ds(0, LANES)
    mine = pl.ds(col * share, share)
    x_main = [
        copy(strips.at[0:3, :, :, cols(p)], ext.at[0:3, mine, 0:ROWS, main], x_ss.at[d], x_rs.at[d], {"lon": p})
        for d, p in others(1)
    ]
    x_heat = [
        copy(strips.at[3, :, :, cols(p)], ext.at[3, mine, 0:ROWS, main], hx_ss.at[d], hx_rs.at[d], {"lon": p})
        for d, p in others(1)
    ]
    rows_n = [
        copy(
            strips.at[:, :, 5:8, cols(p)], ext.at[:, mine, 13:16, main], n_ss.at[d], n_rs.at[d], dict(to_n, lon=p)
        )
        for d, p in others(0)
    ]
    rows_s = [
        copy(
            strips.at[:, :, 0:2, cols(p)], ext.at[:, mine, 8:10, main], s_ss.at[d], s_rs.at[d], dict(to_s, lon=p)
        )
        for d, p in others(0)
    ]
    edges_x = [
        copy(edge_s.at[p], edge_x.at[col, 0:ROWS], ex_ss.at[d], ex_rs.at[d], {"lon": p}) for d, p in others(1)
    ]
    edges_n = [
        copy(edge_s.at[p, 5:8], edge_x.at[col, 13:16], en_ss.at[d], en_rs.at[d], dict(to_n, lon=p))
        for d, p in others(0)
    ]
    edges_s = [
        copy(edge_s.at[p, 0:2], edge_x.at[col, 8:10], es_ss.at[d], es_rs.at[d], dict(to_s, lon=p))
        for d, p in others(0)
    ]
    depth_n = [copy(n_hbm.at[6:8], cnt.at[14:16], k_ss.at[0], k_rs.at[0], to_n)]
    depth_s = [copy(n_hbm.at[0:2], cnt.at[8:10], k_ss.at[1], k_rs.at[1], to_s)]
    near_n = [copy(c_hbm.at[:, :, 7, :], row_s.at[0], c_ss.at[0], c_rs.at[0], to_n)]
    near_s = [copy(c_hbm.at[:, :, 0, :], row_n.at[0], c_ss.at[1], c_rs.at[1], to_s)]
    far_n = [copy(c_hbm.at[:, :, 6, :], row_s.at[1], c_ss.at[2], c_rs.at[2], to_n)]
    far_s = [copy(c_hbm.at[:, :, 1, :], row_n.at[1], c_ss.at[3], c_rs.at[3], to_s)]
    edge_e = [copy(col_ed, got_w, c_ss.at[4], c_rs.at[4], {"lon": lon_e})]
    edge_w = [copy(col_ed, got_e, c_ss.at[5], c_rs.at[5], {"lon": lon_w})]
    corners = [
        (copy(col_ed.at[:, 7, :], cor.at[1, 1], q_ss.at[0], q_rs.at[0], dict(to_n, lon=lon_e)), has_n & has_e, has_s & has_w),
        (copy(col_ed.at[:, 7, :], cor.at[1, 0], q_ss.at[1], q_rs.at[1], dict(to_n, lon=lon_w)), has_n & has_w, has_s & has_e),
        (copy(col_ed.at[:, 0, :], cor.at[0, 1], q_ss.at[2], q_rs.at[2], dict(to_s, lon=lon_e)), has_s & has_e, has_n & has_w),
        (copy(col_ed.at[:, 0, :], cor.at[0, 0], q_ss.at[3], q_rs.at[3], dict(to_s, lon=lon_w)), has_s & has_w, has_n & has_e),
    ]
    flow_out = [
        copy(o_send.at[0:2, pl.ds(p * share, share)], out.at[0:2, :, :, cols(col)], uv_ss.at[d], uv_rs.at[d], {"lon": p})
        for d, p in others(1)
    ]
    warm_out = [
        copy(o_send.at[2, pl.ds(p * share, share)], out.at[2, :, :, cols(col)], t_ss.at[d], t_rs.at[d], {"lon": p})
        for d, p in others(1)
    ]
    heat_out = [
        copy(o_send.at[3, pl.ds(p * share, share)], out.at[3, :, :, cols(col)], h_ss.at[d], h_rs.at[d], {"lon": p})
        for d, p in others(1)
    ]

    lane = lax.broadcasted_iota(jnp.int32, (ROWS, LANES), 1)
    row = lax.broadcasted_iota(jnp.int32, (ROWS, LANES), 0)
    eastern, western = lane % STEP == 0, lane % STEP == STEP - 1

    for load in loads[:4]:
        load.wait()
    for p in range(nlon):
        acc = jnp.zeros((ROWS, LANES), F32)
        for f in range(4):
            for l in range(share):
                g = GROUP * (f * share + l)
                e = strips[f, l, :, (p + 1) * LANES : (p + 2) * LANES] if p < nlon - 1 else jnp.zeros((ROWS, LANES), F32)
                w = strips[f, l, :, (p - 1) * LANES : p * LANES] if p > 0 else jnp.zeros((ROWS, LANES), F32)
                both = jnp.where(lane < LANES // 2, e, w)
                acc = jnp.where((lane + (3 + LANES - g)) % LANES < 5, pltpu.roll(both, g, 1), acc)
        edge_s[p] = acc

    pl.semaphore_wait(barrier, nlon - 1 + nlon * (jnp.minimum(s, 1) + jnp.minimum(nstrip - 1 - s, 1)))
    start(None, x_main)
    start(has_n, rows_n + edges_n + depth_n)
    start(has_s, rows_s + edges_s + depth_s)
    start(None, edges_x + x_heat)
    start(has_n, near_n)
    start(has_s, near_s)

    loads[5].wait()
    for k in range(depth):
        acc = c_in[0, k]
        for t in range(1, tracers):
            here = (lane >= STEP * t - 2) & (lane < STEP * t + 2)
            acc = jnp.where(here, pltpu.roll(c_in[t, k], STEP * t, 1), acc)
        col_ed[k] = acc
    start(has_e, edge_e)
    start(has_w, edge_w)
    for c, send, _ in corners:
        start(send, [c])
    start(has_n, far_n)
    start(has_s, far_s)

    @pl.when(jnp.logical_not(has_s))
    def _():
        ext[:, :, 13:16, 0:LANES] = jnp.zeros((4, depth, 3, LANES), F32)
        edge_x[:, 13:16, :] = jnp.zeros((nlon, 3, LANES), F32)
        cnt[14:16, :] = jnp.zeros((2, nlon * LANES), jnp.int32)
        row_s[...] = jnp.zeros_like(row_s)

    @pl.when(jnp.logical_not(has_n))
    def _():
        ext[:, :, 8:10, 0:LANES] = jnp.zeros((4, depth, 2, LANES), F32)
        edge_x[:, 8:10, :] = jnp.zeros((nlon, 2, LANES), F32)
        cnt[8:10, :] = jnp.zeros((2, nlon * LANES), jnp.int32)
        row_n[...] = jnp.zeros_like(row_n)

    @pl.when(jnp.logical_not(has_w))
    def _():
        got_w[...] = jnp.zeros_like(got_w)

    @pl.when(jnp.logical_not(has_e))
    def _():
        got_e[...] = jnp.zeros_like(got_e)

    for i, there in enumerate((has_n, has_s)):
        for j, beside in enumerate((has_e, has_w)):

            @pl.when(jnp.logical_not(there & beside))
            def _(i=i, j=j):
                cor[i, j] = jnp.zeros((depth, LANES), F32)

    loads[4].wait()
    loads[6].wait()
    for f in range(4):
        ext[f, mine, 0:ROWS, 0:LANES] = strips[f, :, :, cols(col)]
    edge_x[col, 0:ROWS] = edge_s[col]

    high = tracers * ROWS
    spread = (
        lax.broadcasted_iota(jnp.int32, (high, tracers), 0) // ROWS
        == lax.broadcasted_iota(jnp.int32, (high, tracers), 1)
    ).astype(F32)
    gather = (
        lax.broadcasted_iota(jnp.int32, (tracers, high), 1) // ROWS
        == lax.broadcasted_iota(jnp.int32, (tracers, high), 0)
    ).astype(F32)
    rates = jnp.dot(
        spread, jnp.dot(r_in[...], gather, precision=EXACT, preferred_element_type=F32),
        precision=EXACT, preferred_element_type=F32,
    )
    same_row = (
        lax.broadcasted_iota(jnp.int32, (high, high), 0) % ROWS
        == lax.broadcasted_iota(jnp.int32, (high, high), 1) % ROWS
    )
    rates = split(jnp.where(same_row, rates, 0.0))
    spot0 = lax.broadcasted_iota(jnp.int32, (LANES, tracers), 0)
    pick0 = ((spot0 + 1) % LANES // STEP == lax.broadcasted_iota(jnp.int32, (LANES, tracers), 1)).astype(F32)
    spot1 = lax.broadcasted_iota(jnp.int32, (tracers, LANES), 1)
    pick1 = ((spot1 + 1) % LANES // STEP == lax.broadcasted_iota(jnp.int32, (tracers, LANES), 0)).astype(F32)
    across = jnp.dot(
        lax.dot_general(
            pick0, r_in[...], (((1,), (1,)), ((), ())), precision=EXACT, preferred_element_type=F32
        ),
        pick1, precision=EXACT, preferred_element_type=F32,
    )
    side_a = lax.broadcasted_iota(jnp.int32, (LANES, LANES), 0) % STEP
    side_b = lax.broadcasted_iota(jnp.int32, (LANES, LANES), 1) % STEP
    across = split(jnp.where((side_a == side_b) & ((side_a == 0) | (side_a == STEP - 1)), across, 0.0))

    wait_recv(has_s, rows_n + edges_n + depth_n)
    wait_recv(has_n, rows_s + edges_s + depth_s)
    wait_recv(None, x_main + edges_x + x_heat)

    lane2 = lax.broadcasted_iota(jnp.int32, (EXT, LANES), 1)
    window = (lane2 < 2) | (lane2 >= LANES - 3)
    for q in range(nlon):
        held = edge_x[q]
        for f in range(4):
            for l in range(share):
                g = GROUP * (f * share + l)
                moved = pltpu.roll(held, (LANES - g) % LANES, 1) if g else held
                ext[f, q * share + l, :, LANES:WIDE] = jnp.where(window, moved, 0.0)
    wet_e = jnp.where((lane2 < 2) & has_e, cnt[:, cols(lon_e)], 0)
    wet_w = jnp.where((lane2 >= LANES - 3) & has_w, cnt[:, cols(lon_w)], 0)
    n_main = cnt[:, cols(col)]
    n_side = jnp.where(lane2 < LANES // 2, wet_e, wet_w)
    layers = jnp.concatenate([n_main, n_side], axis=1)
    level_main = n_main[0:ROWS]

    line = lax.broadcasted_iota(jnp.int32, (EXT, WIDE), 0)
    spot = (s * ROWS + jnp.where(line < 12, line, line - EXT)).astype(F32)
    fcor = 0.3 * (2.0 * (spot + 0.5) / (nstrip * ROWS) - 1.0)

    for k in range(depth):
        wet = (k < layers).astype(F32)
        wet_u = wet * east(wet)
        wet_v = wet * north(wet)

        def advance(u, v, t):
            new_u = wet_u * (u + 0.1 * lap(u) + fcor * v - 0.2 * (east(t) - t))
            new_v = wet_v * (v + 0.1 * lap(v) - fcor * u - 0.2 * (north(t) - t))
            return new_u, new_v

        u0, v0, t0, h0 = ext[0, k], ext[1, k], ext[2, k], ext[3, k]
        u1, v1 = advance(u0, v0, t0)
        for i, a in enumerate(upwind(u1, west(u1), v1, south(v1))):
            cex[i, k] = a[:, 0:LANES]
            cec[i, k] = a[0:ROWS, LANES:WIDE]
        t1 = wet * (t0 + 0.1 * lap(t0) + 0.5 * h0)
        u2, v2 = advance(u1, v1, t1)
        u_here, v_here = u2[0:ROWS, 0:LANES], v2[0:ROWS, 0:LANES]
        u_back, v_back = west(u2)[0:ROWS, 0:LANES], south(v2)[0:ROWS, 0:LANES]
        for i, a in enumerate(upwind(u_here, u_back, v_here, v_back)):
            cf1[i, k] = a
        t_base[k] = (wet * (t1 + 0.1 * lap(t1)))[0:ROWS, 0:LANES]
        o_send[0, k] = u_here
        o_send[1, k] = v_here
    start(None, flow_out)
    out[0:2, :, :, cols(col)] = o_send[0:2, mine]

    def sides_of(x):
        return jnp.where(eastern, pltpu.roll(x, 1, 1), pltpu.roll(x, LANES - 1, 1))

    def tile_step(m, source, target, above, below, beside):
        def coefs(k):
            if m == 0:
                return [cex[i, k, 0:ROWS, :] for i in range(5)]
            return [cf1[i, k] for i in range(5)]

        def advect(k, t, a, side):
            x = source[t, k]
            edge = pltpu.roll(side, (LANES - STEP * t) % LANES, 1)
            x_n = jnp.where(row == ROWS - 1, above(t, k), pltpu.roll(x, ROWS - 1, 0))
            x_s = jnp.where(row == 0, below(t, k), pltpu.roll(x, 1, 0))
            x_e = jnp.where(lane == LANES - 1, edge, pltpu.roll(x, LANES - 1, 1))
            x_w = jnp.where(lane == 0, edge, pltpu.roll(x, 1, 1))
            return mix(a, x, x_e, x_w, x_n, x_s)

        light, state = {}, [jnp.zeros((ROWS, LANES), F32), jnp.ones((ROWS, LANES), F32)]

        def shine(k):
            lead = advect(k, 0, coefs(k), sides_of(beside(k)))
            wet_k = (k < level_main).astype(F32)
            tau, top = state
            tau = tau + (0.1 + 0.3 * jnp.maximum(lead, 0.0))
            under = jnp.exp(-tau)
            heat = 2.0 * wet_k * (top - under)
            if m == 0:
                o_send[2, k] = t_base[k] + 0.5 * wet_k * heat
            else:
                o_send[3, k] = heat
            light[k] = (lead, wet_k, top)
            state[:] = [tau, under]
            if k == depth - 1:
                start(None, warm_out if m == 0 else heat_out)
                out[2 + m, :, :, cols(col)] = o_send[2 + m, mine]

        groups = depth // PAIR
        held = {}
        if m:
            for k in range(depth):
                shine(k)
        for g in range(groups + 1):
            if g < groups:
                levels = range(g * PAIR, (g + 1) * PAIR)
                adv = []
                for k in levels:
                    if m == 0:
                        shine(k)
                    a, side = coefs(k), sides_of(beside(k))
                    adv.append(
                        jnp.concatenate([light[k][0]] + [advect(k, t, a, side) for t in range(1, tracers)], axis=0)
                    )
                parts = [split(a) for a in adv]
                held[g] = (
                    adv, (jnp.concatenate([a for a, _ in parts], axis=1), jnp.concatenate([b for _, b in parts], axis=1))
                )
            if g > 0:
                adv, both = held.pop(g - 1)
                r = product(rates, both)
                for n in range(PAIR):
                    k = (g - 1) * PAIR + n
                    _, wet_k, top = light[k]
                    gain = r[:, n * LANES : (n + 1) * LANES].reshape(tracers, ROWS, LANES)
                    target[:, k] = wet_k * (adv[n].reshape(tracers, ROWS, LANES) + (0.5 * top) * gain)

    def sideways(k):
        return jnp.where(lane % STEP < 2, got_e[k], got_w[k])

    def ring_rows():
        adv, tops = [], []
        for i in range(2):
            rows, line_at, inner = (row_n, 8, 7) if i == 0 else (row_s, 15, 0)
            a = [cex[j, :, line_at, :] for j in range(5)]
            corner = sides_of(jnp.where(lane % STEP < 2, cor[i, 0], cor[i, 1]))
            values = []
            for t in range(tracers):
                x, far, near = rows[0, t], rows[1, t], c_in[t, :, inner, :]
                edge = pltpu.roll(corner, (LANES - STEP * t) % LANES, 1)
                x_e = jnp.where(lane == LANES - 1, edge, pltpu.roll(x, LANES - 1, 1))
                x_w = jnp.where(lane == 0, edge, pltpu.roll(x, 1, 1))
                x_n, x_s = (far, near) if i == 0 else (near, far)
                values.append(mix(a, x, x_e, x_w, x_n, x_s))
            tau = 0.1 + 0.3 * jnp.maximum(values[0], 0.0)
            tau = jnp.where(row > 0, pltpu.roll(tau, 1, 0), 0.0)
            for shift in (1, 2, 4):
                tau = tau + jnp.where(row >= shift, pltpu.roll(tau, shift, 0), 0.0)
            tops.append(jnp.exp(-tau))
            adv.append(jnp.concatenate(values, axis=0))
        parts = [split(a) for a in adv]
        r = product(
            rates, (jnp.concatenate([a for a, _ in parts], axis=1), jnp.concatenate([b for _, b in parts], axis=1))
        )
        for i, (ring, line_at) in enumerate(((ring_n, 8), (ring_s, 15))):
            wet = (row < n_main[line_at : line_at + 1, :]).astype(F32)
            gain = r[:, i * LANES : (i + 1) * LANES].reshape(tracers, ROWS, LANES)
            ring[...] = wet * (adv[i].reshape(tracers, ROWS, LANES) + (0.5 * tops[i]) * gain)

    def ring_cols():
        def both(x):
            return jnp.where(
                eastern, jnp.broadcast_to(x[:, 0:1], x.shape), jnp.broadcast_to(x[:, LANES - 1 :], x.shape)
            )

        edge_n = jnp.where(lane % STEP < 2, cor[0, 0], cor[0, 1])
        edge_s = jnp.where(lane % STEP < 2, cor[1, 0], cor[1, 1])
        wet_n = both(n_side[0:ROWS])
        tau = jnp.zeros((ROWS, LANES), F32)
        values, tops = [], []
        for k in range(depth):
            x, own = sideways(k), col_ed[k]
            a = [both(cec[i, k]) for i in range(5)]
            x_e = pltpu.roll(jnp.where(eastern, own, x), LANES - 1, 1)
            x_w = pltpu.roll(jnp.where(western, own, x), 1, 1)
            x_n = jnp.where(row == ROWS - 1, edge_n[k : k + 1, :], pltpu.roll(x, ROWS - 1, 0))
            x_s = jnp.where(row == 0, edge_s[k : k + 1, :], pltpu.roll(x, 1, 0))
            value = mix(a, x, x_e, x_w, x_n, x_s)
            values.append(value)
            tops.append(jnp.exp(-tau))
            tau = tau + (0.1 + 0.3 * jnp.maximum(both(value), 0.0))
        r = product(split(jnp.concatenate(values, axis=0)), across)
        for k in range(depth):
            wet = (k < wet_n).astype(F32)
            ring_c[k] = wet * (values[k] + (0.5 * tops[k]) * r[k * ROWS : (k + 1) * ROWS])

    wait_recv(has_s, near_n)
    wait_recv(has_n, near_s)
    wait_recv(has_w, edge_e)
    wait_recv(has_e, edge_w)
    tile_step(
        0, c_in, c_mid,
        lambda t, k: row_n[0, t, k : k + 1, :], lambda t, k: row_s[0, t, k : k + 1, :], sideways,
    )
    wait_recv(has_s, far_n)
    wait_recv(has_n, far_s)
    for c, _, recv in corners:
        wait_recv(recv, [c])
    ring_rows()
    ring_cols()
    tile_step(
        1, c_mid, c_out,
        lambda t, k: ring_n[t, k : k + 1, :], lambda t, k: ring_s[t, k : k + 1, :], lambda k: ring_c[k],
    )

    wait_send(None, x_main + x_heat + edges_x)
    wait_send(has_n, rows_n + edges_n + depth_n + near_n + far_n)
    wait_send(has_s, rows_s + edges_s + depth_s + near_s + far_s)
    wait_send(has_e, edge_e)
    wait_send(has_w, edge_w)
    for c, send, _ in corners:
        wait_send(send, [c])
    wait_send(None, flow_out + warm_out)
    wait_recv(None, flow_out + warm_out)
    wait_send(None, heat_out)
    wait_recv(None, heat_out)


def store(out, c_out, u_dst, v_dst, t_dst, h_dst, c_dst, sem):
    saves = [pltpu.make_async_copy(c_out, c_dst, sem.at[4])]
    saves += [pltpu.make_async_copy(out.at[i], b, sem.at[i]) for i, b in enumerate((u_dst, v_dst, t_dst, h_dst))]
    for save in saves:
        save.start()
    for save in saves:
        save.wait()


def shards(sizes, u, v, t, h, c, n, r):
    tracers, depth, share, nlon, _, _ = sizes
    width = nlon * LANES
    strip = jax.ShapeDtypeStruct(u.shape, F32)
    tile = (ROWS, LANES)
    dma = pltpu.SemaphoreType.DMA
    hbm = pl.BlockSpec(memory_space=pltpu.HBM)
    vmem = pl.BlockSpec(memory_space=pltpu.VMEM)
    buf = pltpu.VMEM
    line = (tracers, depth, LANES)
    pair = [dma((nlon,)), dma((nlon,))]
    held = pl.pallas_call(
        functools.partial(kernel, sizes),
        out_shape=(buf((4, share, ROWS, width), F32), buf(c.shape, F32)),
        in_specs=[hbm] * 7,
        out_specs=(vmem, vmem),
        scratch_shapes=[
            buf((4, share, ROWS, width), F32),
            buf((4, depth, EXT, WIDE), F32),
            buf((nlon,) + tile, F32),
            buf((nlon, EXT, LANES), F32),
            buf((EXT, width), jnp.int32),
            buf(c.shape, F32), buf(c.shape, F32),
            buf((2,) + line, F32), buf((2,) + line, F32), buf(line, F32), buf(line, F32),
            buf((depth,) + tile, F32), buf((depth,) + tile, F32), buf((depth,) + tile, F32),
            buf((2, 2, depth, LANES), F32),
            buf((depth,) + tile, F32),
            buf((5, depth, EXT, LANES), F32),
            buf((5, depth) + tile, F32),
            buf((5, depth) + tile, F32),
            buf((depth,) + tile, F32),
            buf((4, depth) + tile, F32),
            buf(r.shape, F32),
            dma((7,)),
            *(pair * 7),
            dma((2,)), dma((2,)), dma((6,)), dma((6,)), dma((4,)), dma((4,)),
            *(pair * 3),
        ],
        compiler_params=pltpu.CompilerParams(
            collective_id=0, has_side_effects=True, vmem_limit_bytes=VMEM
        ),
    )(*(pltpu.with_memory_space_constraint(x, pltpu.HBM) for x in (u, v, t, h, c, n, r)))
    return pl.pallas_call(
        store,
        out_shape=(strip, strip, strip, strip, jax.ShapeDtypeStruct(c.shape, F32)),
        in_specs=[vmem] * 2,
        out_specs=(hbm,) * 5,
        scratch_shapes=[dma((5,))],
        compiler_params=pltpu.CompilerParams(vmem_limit_bytes=VMEM),
    )(*held)


def solution(mesh):
    nlon, nrole = mesh.shape["lon"], mesh.shape["role"]
    nstrip = mesh.shape["lat"] * nrole
    strip = P("lon", ("grp", "lat", "role"), None)
    tile = P(None, None, ("grp", "lat", "role"), "lon")

    def run(u, v, t, h, c, n, r):
        sizes = (c.shape[0], c.shape[1], u.shape[0] // nlon, nlon, nrole, nstrip)
        return jax.shard_map(
            functools.partial(shards, sizes),
            mesh=mesh,
            in_specs=(strip, strip, strip, strip, tile, P(("grp", "lat", "role"), None), P()),
            out_specs=(strip, strip, strip, strip, tile),
            check_vma=False,
        )(u, v, t, h, c, n, r)

    return run
```

time: 17.5 us -> 16.3 us (0.931)
  Pallas kernels: 16.7 us -> 15.5 us
    pallas_call x1, Pallas kernels: 15.7 us -> 14.6 us  [shards(): pl.pallas_call(functools.partial(kernel, sizes), out_shape=(buf((4, share...]
where the time goes in v1:
time: 16.3 us; the launch traced here: 16.2 us
  Pallas kernels  15.5 us (95%)
  between operations  0.64 us (4%)
    pallas_call x1, Pallas kernels, shards(): pl.pallas_call(functools.partial(kernel, sizes), out_shape=(buf((4, share...  14.6 us
    pallas_call x1, Pallas kernels, shards(): pl.pallas_call(store, out_shape=(strip, strip, strip, strip, jax.ShapeDty...  0.95 us

profile of v1, /device:TPU:0, one launch (start us, length us, event | category | flops | bytes accessed | tf_op | source)
XLA Modules:
  0.0 16.2 jit_solution(589617599644795365)
XLA Ops:
  0.6 14.6 %shard_map.110 = (f32[4,4,8,256]{3,2,1,0:T(8,128)S(1)}, f32[24,8,8,128]{3,2,1,0:T(8,128)S(1)}) custom-call(f32[4,8,256]{2,1,0:T(8,128)} %u_hbm.1, f32[4,8,256]{2,1,0:T(8,128)} %v_hbm.1, f32[4,8,256]{2,1,0:T(8,128)} %t_hbm.1, f32[4,8,256]{2,1,0:T(8,128)} %h_hbm.1, f32[24,8,8,128]{3,2,1,0:T(8,128)} %c_hbm.1, s32[8,256]{1,0:T(8,128)} %n_hbm.1, f32[24,24]{1,0:T(8,128)} %r_hbm.1), custom_call_target="tpu_custom_call" | custom-call | tf_op jit(solution)/shard_map/pallas_call | solution.py:541
  15.2 1.0 %shard_map.111 = (f32[4,8,256]{2,1,0:T(8,128)}, f32[4,8,256]{2,1,0:T(8,128)}, f32[4,8,256]{2,1,0:T(8,128)}, f32[4,8,256]{2,1,0:T(8,128)}, f32[24,8,8,128]{3,2,1,0:T(8,128)}) custom-call(f32[4,4,8,256]{3,2,1,0:T(8,128)S(1)} %get-tuple-element.7.out, f32[24,8,8,128]{3,2,1,0:T(8,128)S(1)} %get-tuple-element.8.c_out), custom_call_target="tpu_custom_call" | custom-call | tf_op jit(solution)/shard_map/pallas_call | solution.py:572

commit v2 on v1

--- a/solution.py
+++ b/solution.py
@@ -57,6 +57,10 @@
     return hi, (a - hi.astype(F32)).astype(jnp.bfloat16)
 
 
+def halves(a):
+    return jnp.concatenate(split(a), axis=1)
+
+
 def product(a, b):
     a_hi, a_lo = a
     b_hi, b_lo = b
@@ -71,17 +75,29 @@
     sizes,
     u_hbm, v_hbm, t_hbm, h_hbm, c_hbm, n_hbm, r_hbm,
     out, c_out,
-    strips, ext, edge_s, edge_x, cnt, c_in, c_mid, row_n, row_s, ring_n, ring_s,
-    col_ed, got_e, got_w, cor, ring_c, cex, cec, cf1, t_base, o_send, r_in, in_sem,
-    x_ss, x_rs, hx_ss, hx_rs, n_ss, n_rs, s_ss, s_rs, ex_ss, ex_rs, en_ss, en_rs, es_ss, es_rs,
+    stage, tall, flow, cnt, c_in, c_raw, c_mid, row_n, row_s, raw_n, raw_s, ring_n, ring_s,
+    col_ed, got_e, got_w, cor, ring_c, lead_c, lead_n, lead_s, cex, cec, cf1, t_base, o_send, r_in, in_sem, strip_sem,
+    x_ss, x_rs, hx_ss, hx_rs, n_ss, n_rs, s_ss, s_rs,
     k_ss, k_rs, c_ss, c_rs, q_ss, q_rs, uv_ss, uv_rs, t_ss, t_rs, h_ss, h_rs,
 ):
     tracers, depth, share, nlon, nrole, nstrip = sizes
-    loads = [pltpu.make_async_copy(a, strips.at[i], in_sem.at[i]) for i, a in enumerate((u_hbm, v_hbm, t_hbm, h_hbm))]
-    loads.append(pltpu.make_async_copy(n_hbm, cnt.at[0:ROWS], in_sem.at[4]))
-    loads.append(pltpu.make_async_copy(c_hbm, c_in, in_sem.at[5]))
-    loads.append(pltpu.make_async_copy(r_hbm, r_in, in_sem.at[6]))
-    for load in loads:
+    early = 3 * share + 1
+
+    def slot(f, l):
+        return f * share + l + (f == 3)
+
+    strip_loads = [
+        pltpu.make_async_copy(
+            a.at[:, :, p * LANES : (p + 1) * LANES], stage.at[p, slot(f, 0) : slot(f, 0) + share], strip_sem.at[f, p]
+        )
+        for f, a in enumerate((u_hbm, v_hbm, t_hbm, h_hbm))
+        for p in range(nlon)
+    ]
+    loads = [
+        pltpu.make_async_copy(a, b, in_sem.at[i])
+        for i, (a, b) in enumerate(((n_hbm, cnt.at[0:ROWS]), (c_hbm, c_in), (r_hbm, r_in)))
+    ]
+    for load in strip_loads + loads:
         load.start()
 
     s = lax.axis_index("lat") * nrole + lax.axis_index("role")
@@ -144,37 +160,24 @@
     def cols(p):
         return pl.ds(pl.multiple_of(p * LANES, LANES), LANES)
 
-    main = pl.ds(0, LANES)
     mine = pl.ds(col * share, share)
     x_main = [
-        copy(strips.at[0:3, :, :, cols(p)], ext.at[0:3, mine, 0:ROWS, main], x_ss.at[d], x_rs.at[d], {"lon": p})
+        copy(stage.at[p, 0:early], tall.at[col, 0:early, 0:ROWS], x_ss.at[d], x_rs.at[d], {"lon": p})
         for d, p in others(1)
     ]
     x_heat = [
-        copy(strips.at[3, :, :, cols(p)], ext.at[3, mine, 0:ROWS, main], hx_ss.at[d], hx_rs.at[d], {"lon": p})
+        copy(
+            stage.at[p, early : early + share], tall.at[col, early : early + share, 0:ROWS],
+            hx_ss.at[d], hx_rs.at[d], {"lon": p},
+        )
         for d, p in others(1)
     ]
     rows_n = [
-        copy(
-            strips.at[:, :, 5:8, cols(p)], ext.at[:, mine, 13:16, main], n_ss.at[d], n_rs.at[d], dict(to_n, lon=p)
-        )
+        copy(stage.at[p, :, 5:8], tall.at[col, :, 13:16], n_ss.at[d], n_rs.at[d], dict(to_n, lon=p))
         for d, p in others(0)
     ]
     rows_s = [
-        copy(
-            strips.at[:, :, 0:2, cols(p)], ext.at[:, mine, 8:10, main], s_ss.at[d], s_rs.at[d], dict(to_s, lon=p)
-        )
-        for d, p in others(0)
-    ]
-    edges_x = [
-        copy(edge_s.at[p], edge_x.at[col, 0:ROWS], ex_ss.at[d], ex_rs.at[d], {"lon": p}) for d, p in others(1)
-    ]
-    edges_n = [
-        copy(edge_s.at[p, 5:8], edge_x.at[col, 13:16], en_ss.at[d], en_rs.at[d], dict(to_n, lon=p))
-        for d, p in others(0)
-    ]
-    edges_s = [
-        copy(edge_s.at[p, 0:2], edge_x.at[col, 8:10], es_ss.at[d], es_rs.at[d], dict(to_s, lon=p))
+        copy(stage.at[p, :, 0:2], tall.at[col, :, 8:10], s_ss.at[d], s_rs.at[d], dict(to_s, lon=p))
         for d, p in others(0)
     ]
     depth_n = [copy(n_hbm.at[6:8], cnt.at[14:16], k_ss.at[0], k_rs.at[0], to_n)]
@@ -208,33 +211,59 @@
     row = lax.broadcasted_iota(jnp.int32, (ROWS, LANES), 0)
     eastern, western = lane % STEP == 0, lane % STEP == STEP - 1
 
-    for load in loads[:4]:
+    def spots(axis):
+        return lax.broadcasted_iota(jnp.int32, (LANES, LANES), axis)
+
+    def twice(mask):
+        one = mask.astype(F32).astype(jnp.bfloat16)
+        return jnp.concatenate([one, one], axis=0)
+
+    far_lane = (spots(1) + STEP // 2) % STEP
+    take = twice(spots(0) == (far_lane + LANES - STEP // 2) % LANES)
+    give = twice(
+        ((spots(0) % STEP == 0) & (spots(1) == LANES - 1)) | ((spots(0) % STEP == STEP - 1) & (spots(1) == 0))
+    )
+
+    def unpack(a, b):
+        parts = halves(jnp.concatenate([a, b], axis=0))
+        place = lax.broadcasted_iota(jnp.int32, (1, WIDE), 1) % LANES
+        only = [
+            ((place + 1) % LANES // STEP == t).astype(F32).astype(jnp.bfloat16) for t in range(tracers)
+        ]
+        e = jnp.dot(jnp.concatenate([parts * o for o in only], axis=0), give, preferred_element_type=F32)
+        return [[e[(2 * t + i) * ROWS : (2 * t + i + 1) * ROWS] for i in range(2)] for t in range(tracers)]
+
+    for load in strip_loads:
         load.wait()
+    blank = jnp.zeros((ROWS, LANES), F32)
     for p in range(nlon):
-        acc = jnp.zeros((ROWS, LANES), F32)
+        acc = blank
         for f in range(4):
             for l in range(share):
                 g = GROUP * (f * share + l)
-                e = strips[f, l, :, (p + 1) * LANES : (p + 2) * LANES] if p < nlon - 1 else jnp.zeros((ROWS, LANES), F32)
-                w = strips[f, l, :, (p - 1) * LANES : p * LANES] if p > 0 else jnp.zeros((ROWS, LANES), F32)
+                e = stage[p + 1, slot(f, l)] if p < nlon - 1 else blank
+                w = stage[p - 1, slot(f, l)] if p > 0 else blank
                 both = jnp.where(lane < LANES // 2, e, w)
                 acc = jnp.where((lane + (3 + LANES - g)) % LANES < 5, pltpu.roll(both, g, 1), acc)
-        edge_s[p] = acc
+        stage[p, 3 * share] = acc
 
     pl.semaphore_wait(barrier, nlon - 1 + nlon * (jnp.minimum(s, 1) + jnp.minimum(nstrip - 1 - s, 1)))
+    start(has_n, rows_n[::-1] + depth_n)
+    start(has_s, rows_s[::-1] + depth_s)
     start(None, x_main)
-    start(has_n, rows_n + edges_n + depth_n)
-    start(has_s, rows_s + edges_s + depth_s)
-    start(None, edges_x + x_heat)
     start(has_n, near_n)
     start(has_s, near_s)
-
-    loads[5].wait()
+    start(None, x_heat)
+
+    loads[1].wait()
     for k in range(depth):
-        acc = c_in[0, k]
+        picked = jnp.dot(
+            jnp.concatenate([halves(c_in[t, k]) for t in range(tracers)], axis=0), take, preferred_element_type=F32
+        )
+        acc = picked[0:ROWS]
         for t in range(1, tracers):
             here = (lane >= STEP * t - 2) & (lane < STEP * t + 2)
-            acc = jnp.where(here, pltpu.roll(c_in[t, k], STEP * t, 1), acc)
+            acc = jnp.where(here, picked[t * ROWS : (t + 1) * ROWS], acc)
         col_ed[k] = acc
     start(has_e, edge_e)
     start(has_w, edge_w)
@@ -245,15 +274,13 @@
 
     @pl.when(jnp.logical_not(has_s))
     def _():
-        ext[:, :, 13:16, 0:LANES] = jnp.zeros((4, depth, 3, LANES), F32)
-        edge_x[:, 13:16, :] = jnp.zeros((nlon, 3, LANES), F32)
+        tall[:, :, 13:16, :] = jnp.zeros((nlon, 4 * share + 1, 3, LANES), F32)
         cnt[14:16, :] = jnp.zeros((2, nlon * LANES), jnp.int32)
         row_s[...] = jnp.zeros_like(row_s)
 
     @pl.when(jnp.logical_not(has_n))
     def _():
-        ext[:, :, 8:10, 0:LANES] = jnp.zeros((4, depth, 2, LANES), F32)
-        edge_x[:, 8:10, :] = jnp.zeros((nlon, 2, LANES), F32)
+        tall[:, :, 8:10, :] = jnp.zeros((nlon, 4 * share + 1, 2, LANES), F32)
         cnt[8:10, :] = jnp.zeros((2, nlon * LANES), jnp.int32)
         row_n[...] = jnp.zeros_like(row_n)
 
@@ -272,11 +299,10 @@
             def _(i=i, j=j):
                 cor[i, j] = jnp.zeros((depth, LANES), F32)
 
-    loads[4].wait()
-    loads[6].wait()
-    for f in range(4):
-        ext[f, mine, 0:ROWS, 0:LANES] = strips[f, :, :, cols(col)]
-    edge_x[col, 0:ROWS] = edge_s[col]
+    loads[0].wait()
+    loads[2].wait()
+    tall[col, :, 0:ROWS] = stage[col]
+    lead_rates = [jnp.broadcast_to(r_in[0:1, b : b + 1], (ROWS, LANES)) for b in range(tracers)]
 
     high = tracers * ROWS
     spread = (
@@ -310,19 +336,20 @@
     side_b = lax.broadcasted_iota(jnp.int32, (LANES, LANES), 1) % STEP
     across = split(jnp.where((side_a == side_b) & ((side_a == 0) | (side_a == STEP - 1)), across, 0.0))
 
-    wait_recv(has_s, rows_n + edges_n + depth_n)
-    wait_recv(has_n, rows_s + edges_s + depth_s)
-    wait_recv(None, x_main + edges_x + x_heat)
+    wait_recv(has_s, rows_n + depth_n)
+    wait_recv(has_n, rows_s + depth_s)
+    wait_recv(None, x_main)
 
     lane2 = lax.broadcasted_iota(jnp.int32, (EXT, LANES), 1)
     window = (lane2 < 2) | (lane2 >= LANES - 3)
-    for q in range(nlon):
-        held = edge_x[q]
-        for f in range(4):
-            for l in range(share):
-                g = GROUP * (f * share + l)
-                moved = pltpu.roll(held, (LANES - g) % LANES, 1) if g else held
-                ext[f, q * share + l, :, LANES:WIDE] = jnp.where(window, moved, 0.0)
+
+    def field(f, k):
+        q, l = k // share, k % share
+        g = GROUP * (f * share + l)
+        held = tall[q, 3 * share]
+        moved = pltpu.roll(held, (LANES - g) % LANES, 1) if g else held
+        return jnp.concatenate([tall[q, slot(f, l)], jnp.where(window, moved, 0.0)], axis=1)
+
     wet_e = jnp.where((lane2 < 2) & has_e, cnt[:, cols(lon_e)], 0)
     wet_w = jnp.where((lane2 >= LANES - 3) & has_w, cnt[:, cols(lon_w)], 0)
     n_main = cnt[:, cols(col)]
@@ -334,57 +361,60 @@
     spot = (s * ROWS + jnp.where(line < 12, line, line - EXT)).astype(F32)
     fcor = 0.3 * (2.0 * (spot + 0.5) / (nstrip * ROWS) - 1.0)
 
+    def masks(k):
+        wet = (k < layers).astype(F32)
+        return wet, wet * east(wet), wet * north(wet)
+
+    def advance(m, u, v, t):
+        new_u = m[1] * (u + 0.1 * lap(u) + fcor * v - 0.2 * (east(t) - t))
+        new_v = m[2] * (v + 0.1 * lap(v) - fcor * u - 0.2 * (north(t) - t))
+        return new_u, new_v
+
     for k in range(depth):
-        wet = (k < layers).astype(F32)
-        wet_u = wet * east(wet)
-        wet_v = wet * north(wet)
-
-        def advance(u, v, t):
-            new_u = wet_u * (u + 0.1 * lap(u) + fcor * v - 0.2 * (east(t) - t))
-            new_v = wet_v * (v + 0.1 * lap(v) - fcor * u - 0.2 * (north(t) - t))
-            return new_u, new_v
-
-        u0, v0, t0, h0 = ext[0, k], ext[1, k], ext[2, k], ext[3, k]
-        u1, v1 = advance(u0, v0, t0)
+        u1, v1 = advance(masks(k), field(0, k), field(1, k), field(2, k))
+        flow[0, k], flow[1, k] = u1, v1
         for i, a in enumerate(upwind(u1, west(u1), v1, south(v1))):
             cex[i, k] = a[:, 0:LANES]
             cec[i, k] = a[0:ROWS, LANES:WIDE]
-        t1 = wet * (t0 + 0.1 * lap(t0) + 0.5 * h0)
-        u2, v2 = advance(u1, v1, t1)
+    wait_recv(None, x_heat)
+    for k in range(depth):
+        m = masks(k)
+        t0 = field(2, k)
+        t1 = m[0] * (t0 + 0.1 * lap(t0) + 0.5 * field(3, k))
+        u2, v2 = advance(m, flow[0, k], flow[1, k], t1)
         u_here, v_here = u2[0:ROWS, 0:LANES], v2[0:ROWS, 0:LANES]
         u_back, v_back = west(u2)[0:ROWS, 0:LANES], south(v2)[0:ROWS, 0:LANES]
         for i, a in enumerate(upwind(u_here, u_back, v_here, v_back)):
             cf1[i, k] = a
-        t_base[k] = (wet * (t1 + 0.1 * lap(t1)))[0:ROWS, 0:LANES]
+        t_base[k] = (m[0] * (t1 + 0.1 * lap(t1)))[0:ROWS, 0:LANES]
         o_send[0, k] = u_here
         o_send[1, k] = v_here
     start(None, flow_out)
     out[0:2, :, :, cols(col)] = o_send[0:2, mine]
 
-    def sides_of(x):
-        return jnp.where(eastern, pltpu.roll(x, 1, 1), pltpu.roll(x, LANES - 1, 1))
-
-    def tile_step(m, source, target, above, below, beside):
-        def coefs(k):
-            if m == 0:
-                return [cex[i, k, 0:ROWS, :] for i in range(5)]
-            return [cf1[i, k] for i in range(5)]
-
-        def advect(k, t, a, side):
-            x = source[t, k]
-            edge = pltpu.roll(side, (LANES - STEP * t) % LANES, 1)
-            x_n = jnp.where(row == ROWS - 1, above(t, k), pltpu.roll(x, ROWS - 1, 0))
-            x_s = jnp.where(row == 0, below(t, k), pltpu.roll(x, 1, 0))
-            x_e = jnp.where(lane == LANES - 1, edge, pltpu.roll(x, LANES - 1, 1))
-            x_w = jnp.where(lane == 0, edge, pltpu.roll(x, 1, 1))
-            return mix(a, x, x_e, x_w, x_n, x_s)
-
-        light, state = {}, [jnp.zeros((ROWS, LANES), F32), jnp.ones((ROWS, LANES), F32)]
-
-        def shine(k):
-            lead = advect(k, 0, coefs(k), sides_of(beside(k)))
+    def coefs(m, k):
+        if m == 0:
+            return [cex[i, k, 0:ROWS, :] for i in range(5)]
+        return [cf1[i, k] for i in range(5)]
+
+    def advect(a, x, edge, above, below):
+        x_n = jnp.where(row == ROWS - 1, above, pltpu.roll(x, ROWS - 1, 0))
+        x_s = jnp.where(row == 0, below, pltpu.roll(x, 1, 0))
+        x_e = jnp.where(lane == LANES - 1, edge, pltpu.roll(x, LANES - 1, 1))
+        x_w = jnp.where(lane == 0, edge, pltpu.roll(x, 1, 1))
+        return mix(a, x, x_e, x_w, x_n, x_s)
+
+    def lead_of(values):
+        parts = [v * a for v, a in zip(values, lead_rates)]
+        while len(parts) > 1:
+            parts = [sum(parts[i : i + 2]) for i in range(0, len(parts), 2)]
+        return parts[0]
+
+    def shine(m, leads):
+        tau, top = jnp.zeros((ROWS, LANES), F32), jnp.ones((ROWS, LANES), F32)
+        tops = []
+        for k, lead in enumerate(leads):
             wet_k = (k < level_main).astype(F32)
-            tau, top = state
             tau = tau + (0.1 + 0.3 * jnp.maximum(lead, 0.0))
             under = jnp.exp(-tau)
             heat = 2.0 * wet_k * (top - under)
@@ -392,72 +422,56 @@
                 o_send[2, k] = t_base[k] + 0.5 * wet_k * heat
             else:
                 o_send[3, k] = heat
-            light[k] = (lead, wet_k, top)
-            state[:] = [tau, under]
-            if k == depth - 1:
-                start(None, warm_out if m == 0 else heat_out)
-                out[2 + m, :, :, cols(col)] = o_send[2 + m, mine]
-
-        groups = depth // PAIR
-        held = {}
-        if m:
-            for k in range(depth):
-                shine(k)
-        for g in range(groups + 1):
-            if g < groups:
-                levels = range(g * PAIR, (g + 1) * PAIR)
-                adv = []
-                for k in levels:
-                    if m == 0:
-                        shine(k)
-                    a, side = coefs(k), sides_of(beside(k))
-                    adv.append(
-                        jnp.concatenate([light[k][0]] + [advect(k, t, a, side) for t in range(1, tracers)], axis=0)
-                    )
-                parts = [split(a) for a in adv]
-                held[g] = (
-                    adv, (jnp.concatenate([a for a, _ in parts], axis=1), jnp.concatenate([b for _, b in parts], axis=1))
-                )
-            if g > 0:
-                adv, both = held.pop(g - 1)
-                r = product(rates, both)
-                for n in range(PAIR):
-                    k = (g - 1) * PAIR + n
-                    _, wet_k, top = light[k]
-                    gain = r[:, n * LANES : (n + 1) * LANES].reshape(tracers, ROWS, LANES)
-                    target[:, k] = wet_k * (adv[n].reshape(tracers, ROWS, LANES) + (0.5 * top) * gain)
+            tops.append(top)
+            top = under
+        start(None, heat_out if m else warm_out)
+        out[2 + m, :, :, cols(col)] = o_send[2 + m, mine]
+        return tops
+
+    def react(blocks):
+        parts = [split(a) for a in blocks]
+        r = product(
+            rates, (jnp.concatenate([a for a, _ in parts], axis=1), jnp.concatenate([b for _, b in parts], axis=1))
+        )
+        return [r[:, i * LANES : (i + 1) * LANES].reshape(tracers, ROWS, LANES) for i in range(len(blocks))]
+
+    def settle(k, top, value, gain):
+        return (k < level_main).astype(F32) * (value + (0.5 * top) * gain)
 
     def sideways(k):
         return jnp.where(lane % STEP < 2, got_e[k], got_w[k])
 
     def ring_rows():
-        adv, tops = [], []
+        tops, wets = [], []
+        ends = unpack(*(jnp.where(lane % STEP < 2, cor[i, 0], cor[i, 1]) for i in range(2)))
         for i in range(2):
             rows, line_at, inner = (row_n, 8, 7) if i == 0 else (row_s, 15, 0)
             a = [cex[j, :, line_at, :] for j in range(5)]
-            corner = sides_of(jnp.where(lane % STEP < 2, cor[i, 0], cor[i, 1]))
             values = []
             for t in range(tracers):
                 x, far, near = rows[0, t], rows[1, t], c_in[t, :, inner, :]
-                edge = pltpu.roll(corner, (LANES - STEP * t) % LANES, 1)
+                edge = ends[t][i]
                 x_e = jnp.where(lane == LANES - 1, edge, pltpu.roll(x, LANES - 1, 1))
                 x_w = jnp.where(lane == 0, edge, pltpu.roll(x, 1, 1))
                 x_n, x_s = (far, near) if i == 0 else (near, far)
                 values.append(mix(a, x, x_e, x_w, x_n, x_s))
+                (raw_n, raw_s)[i][t] = values[t]
             tau = 0.1 + 0.3 * jnp.maximum(values[0], 0.0)
             tau = jnp.where(row > 0, pltpu.roll(tau, 1, 0), 0.0)
             for shift in (1, 2, 4):
                 tau = tau + jnp.where(row >= shift, pltpu.roll(tau, shift, 0), 0.0)
-            tops.append(jnp.exp(-tau))
-            adv.append(jnp.concatenate(values, axis=0))
-        parts = [split(a) for a in adv]
-        r = product(
-            rates, (jnp.concatenate([a for a, _ in parts], axis=1), jnp.concatenate([b for _, b in parts], axis=1))
-        )
-        for i, (ring, line_at) in enumerate(((ring_n, 8), (ring_s, 15))):
+            top = jnp.exp(-tau)
             wet = (row < n_main[line_at : line_at + 1, :]).astype(F32)
-            gain = r[:, i * LANES : (i + 1) * LANES].reshape(tracers, ROWS, LANES)
-            ring[...] = wet * (adv[i].reshape(tracers, ROWS, LANES) + (0.5 * tops[i]) * gain)
+            (lead_n, lead_s)[i][...] = wet * (values[0] + (0.5 * top) * lead_of(values))
+            tops.append(top)
+            wets.append(wet)
+        return tops, wets
+
+    def ring_finish(tops, wets):
+        blocks = [a[...] for a in (raw_n, raw_s)]
+        gains = react([a.reshape(high, LANES) for a in blocks])
+        for i, ring in enumerate((ring_n, ring_s)):
+            ring[...] = wets[i] * (blocks[i] + (0.5 * tops[i]) * gains[i])
 
     def ring_cols():
         def both(x):
@@ -486,28 +500,66 @@
             wet = (k < wet_n).astype(F32)
             ring_c[k] = wet * (values[k] + (0.5 * tops[k]) * r[k * ROWS : (k + 1) * ROWS])
 
+    groups = [range(g, g + PAIR) for g in range(0, depth, PAIR)]
     wait_recv(has_s, near_n)
     wait_recv(has_n, near_s)
     wait_recv(has_w, edge_e)
     wait_recv(has_e, edge_w)
-    tile_step(
-        0, c_in, c_mid,
-        lambda t, k: row_n[0, t, k : k + 1, :], lambda t, k: row_s[0, t, k : k + 1, :], sideways,
-    )
+    leads, firsts = [], []
+    for levels in groups:
+        edges = unpack(*(sideways(k) for k in levels))
+        for i, k in enumerate(levels):
+            a = coefs(0, k)
+            values = [
+                advect(a, c_in[t, k], edges[t][i], row_n[0, t, k : k + 1, :], row_s[0, t, k : k + 1, :])
+                for t in range(tracers)
+            ]
+            for t in range(tracers):
+                c_raw[t, k] = values[t]
+            leads.append(values[0])
+            firsts.append(lead_of(values))
+    tops = shine(0, leads)
+    for k in range(depth):
+        lead_c[k] = settle(k, tops[k], leads[k], firsts[k])
+
     wait_recv(has_s, far_n)
     wait_recv(has_n, far_s)
     for c, _, recv in corners:
         wait_recv(recv, [c])
-    ring_rows()
     ring_cols()
-    tile_step(
-        1, c_mid, c_out,
-        lambda t, k: ring_n[t, k : k + 1, :], lambda t, k: ring_s[t, k : k + 1, :], lambda k: ring_c[k],
-    )
-
-    wait_send(None, x_main + x_heat + edges_x)
-    wait_send(has_n, rows_n + edges_n + depth_n + near_n + far_n)
-    wait_send(has_s, rows_s + edges_s + depth_s + near_s + far_s)
+    ring_light = ring_rows()
+    leads = []
+    for k in range(depth):
+        x, beside = lead_c[k], ring_c[k]
+        x_n = jnp.where(row == ROWS - 1, lead_n[k : k + 1, :], pltpu.roll(x, ROWS - 1, 0))
+        x_s = jnp.where(row == 0, lead_s[k : k + 1, :], pltpu.roll(x, 1, 0))
+        x_e = pltpu.roll(jnp.where(lane == 0, beside, x), LANES - 1, 1)
+        x_w = pltpu.roll(jnp.where(lane == LANES - 1, beside, x), 1, 1)
+        leads.append(mix(coefs(1, k), x, x_e, x_w, x_n, x_s))
+    last = shine(1, leads)
+
+    ring_finish(*ring_light)
+    for levels in groups:
+        blocks = [c_raw[:, k] for k in levels]
+        gains = react([b.reshape(high, LANES) for b in blocks])
+        for k, block, gain in zip(levels, blocks, gains):
+            c_mid[:, k] = settle(k, tops[k], block, gain)
+    for levels in groups:
+        edges = unpack(*(ring_c[k] for k in levels))
+        blocks = []
+        for i, k in enumerate(levels):
+            a = coefs(1, k)
+            blocks.append(jnp.concatenate([leads[k]] + [
+                advect(a, c_mid[t, k], edges[t][i], ring_n[t, k : k + 1, :], ring_s[t, k : k + 1, :])
+                for t in range(1, tracers)
+            ], axis=0))
+        gains = react(blocks)
+        for k, block, gain in zip(levels, blocks, gains):
+            c_out[:, k] = settle(k, last[k], block.reshape(tracers, ROWS, LANES), gain)
+
+    wait_send(None, x_main + x_heat)
+    wait_send(has_n, rows_n + depth_n + near_n + far_n)
+    wait_send(has_s, rows_s + depth_s + near_s + far_s)
     wait_send(has_e, edge_e)
     wait_send(has_w, edge_w)
     for c, send, _ in corners:
@@ -544,24 +596,24 @@
         in_specs=[hbm] * 7,
         out_specs=(vmem, vmem),
         scratch_shapes=[
-            buf((4, share, ROWS, width), F32),
-            buf((4, depth, EXT, WIDE), F32),
-            buf((nlon,) + tile, F32),
-            buf((nlon, EXT, LANES), F32),
+            buf((nlon, 4 * share + 1) + tile, F32),
+            buf((nlon, 4 * share + 1, EXT, LANES), F32),
+            buf((2, depth, EXT, WIDE), F32),
             buf((EXT, width), jnp.int32),
-            buf(c.shape, F32), buf(c.shape, F32),
-            buf((2,) + line, F32), buf((2,) + line, F32), buf(line, F32), buf(line, F32),
+            buf(c.shape, F32), buf(c.shape, F32), buf(c.shape, F32),
+            buf((2,) + line, F32), buf((2,) + line, F32),
+            buf(line, F32), buf(line, F32), buf(line, F32), buf(line, F32),
             buf((depth,) + tile, F32), buf((depth,) + tile, F32), buf((depth,) + tile, F32),
             buf((2, 2, depth, LANES), F32),
-            buf((depth,) + tile, F32),
+            buf((depth,) + tile, F32), buf((depth,) + tile, F32), buf((depth, LANES), F32), buf((depth, LANES), F32),
             buf((5, depth, EXT, LANES), F32),
             buf((5, depth) + tile, F32),
             buf((5, depth) + tile, F32),
             buf((depth,) + tile, F32),
             buf((4, depth) + tile, F32),
             buf(r.shape, F32),
-            dma((7,)),
-            *(pair * 7),
+            dma((3,)), dma((4, nlon)),
+            *(pair * 4),
             dma((2,)), dma((2,)), dma((6,)), dma((6,)), dma((4,)), dma((4,)),
             *(pair * 3),
         ],

time: 16.3 us -> 14.6 us (0.90)
  Pallas kernels: 15.5 us -> 13.8 us
    pallas_call x1, Pallas kernels: 14.6 us -> 12.8 us  [shards(): pl.pallas_call(functools.partial(kernel, sizes), out_shape=(buf((4, share...]
where the time goes in v2:
time: 14.6 us; the launch traced here: 14.4 us
  Pallas kernels  13.8 us (95%)
  between operations  0.64 us (4%)
    pallas_call x1, Pallas kernels, shards(): pl.pallas_call(functools.partial(kernel, sizes), out_shape=(buf((4, share...  12.8 us
    pallas_call x1, Pallas kernels, shards(): pl.pallas_call(store, out_shape=(strip, strip, strip, strip, jax.ShapeDty...  0.95 us

profile of v2, /device:TPU:0, one launch (start us, length us, event | category | flops | bytes accessed | tf_op | source)
XLA Modules:
  0.0 14.4 jit_solution(17850076293780950368)
XLA Ops:
  0.6 12.8 %shard_map.110 = (f32[4,4,8,256]{3,2,1,0:T(8,128)S(1)}, f32[24,8,8,128]{3,2,1,0:T(8,128)S(1)}) custom-call(f32[4,8,256]{2,1,0:T(8,128)} %u_hbm.1, f32[4,8,256]{2,1,0:T(8,128)} %v_hbm.1, f32[4,8,256]{2,1,0:T(8,128)} %t_hbm.1, f32[4,8,256]{2,1,0:T(8,128)} %h_hbm.1, f32[24,8,8,128]{3,2,1,0:T(8,128)} %c_hbm.1, s32[8,256]{1,0:T(8,128)} %n_hbm.1, f32[24,24]{1,0:T(8,128)} %r_hbm.1), custom_call_target="tpu_custom_call" | custom-call | tf_op jit(solution)/shard_map/pallas_call | solution.py:593
  13.5 1.0 %shard_map.111 = (f32[4,8,256]{2,1,0:T(8,128)}, f32[4,8,256]{2,1,0:T(8,128)}, f32[4,8,256]{2,1,0:T(8,128)}, f32[4,8,256]{2,1,0:T(8,128)}, f32[24,8,8,128]{3,2,1,0:T(8,128)}) custom-call(f32[4,4,8,256]{3,2,1,0:T(8,128)S(1)} %get-tuple-element.7.out, f32[24,8,8,128]{3,2,1,0:T(8,128)S(1)} %get-tuple-element.8.c_out), custom_call_target="tpu_custom_call" | custom-call | tf_op jit(solution)/shard_map/pallas_call | solution.py:624

commit v3 on v2

--- a/solution.py
+++ b/solution.py
@@ -76,13 +76,11 @@
     u_hbm, v_hbm, t_hbm, h_hbm, c_hbm, n_hbm, r_hbm,
     out, c_out,
     stage, tall, flow, cnt, c_in, c_raw, c_mid, row_n, row_s, raw_n, raw_s, ring_n, ring_s,
-    col_ed, got_e, got_w, cor, ring_c, lead_c, lead_n, lead_s, cex, cec, cf1, t_base, o_send, r_in, in_sem, strip_sem,
-    x_ss, x_rs, hx_ss, hx_rs, n_ss, n_rs, s_ss, s_rs,
+    col_ed, send_e, send_w, got_e, got_w, cor, ring_c, lead_c, lead_n, lead_s, cex, cec, cf1, t_base, o_send, r_in, in_sem, strip_sem,
+    x_ss, x_rs, n_ss, n_rs, s_ss, s_rs,
     k_ss, k_rs, c_ss, c_rs, q_ss, q_rs, uv_ss, uv_rs, t_ss, t_rs, h_ss, h_rs,
 ):
     tracers, depth, share, nlon, nrole, nstrip = sizes
-    early = 3 * share + 1
-
     def slot(f, l):
         return f * share + l + (f == 3)
 
@@ -162,14 +160,7 @@
 
     mine = pl.ds(col * share, share)
     x_main = [
-        copy(stage.at[p, 0:early], tall.at[col, 0:early, 0:ROWS], x_ss.at[d], x_rs.at[d], {"lon": p})
-        for d, p in others(1)
-    ]
-    x_heat = [
-        copy(
-            stage.at[p, early : early + share], tall.at[col, early : early + share, 0:ROWS],
-            hx_ss.at[d], hx_rs.at[d], {"lon": p},
-        )
+        copy(stage.at[p], tall.at[col, :, 0:ROWS], x_ss.at[d], x_rs.at[d], {"lon": p})
         for d, p in others(1)
     ]
     rows_n = [
@@ -186,8 +177,8 @@
     near_s = [copy(c_hbm.at[:, :, 0, :], row_n.at[0], c_ss.at[1], c_rs.at[1], to_s)]
     far_n = [copy(c_hbm.at[:, :, 6, :], row_s.at[1], c_ss.at[2], c_rs.at[2], to_n)]
     far_s = [copy(c_hbm.at[:, :, 1, :], row_n.at[1], c_ss.at[3], c_rs.at[3], to_s)]
-    edge_e = [copy(col_ed, got_w, c_ss.at[4], c_rs.at[4], {"lon": lon_e})]
-    edge_w = [copy(col_ed, got_e, c_ss.at[5], c_rs.at[5], {"lon": lon_w})]
+    edge_e = [copy(send_e, got_w, c_ss.at[4], c_rs.at[4], {"lon": lon_e})]
+    edge_w = [copy(send_w, got_e, c_ss.at[5], c_rs.at[5], {"lon": lon_w})]
     corners = [
         (copy(col_ed.at[:, 7, :], cor.at[1, 1], q_ss.at[0], q_rs.at[0], dict(to_n, lon=lon_e)), has_n & has_e, has_s & has_w),
         (copy(col_ed.at[:, 7, :], cor.at[1, 0], q_ss.at[1], q_rs.at[1], dict(to_n, lon=lon_w)), has_n & has_w, has_s & has_e),
@@ -253,7 +244,6 @@
     start(None, x_main)
     start(has_n, near_n)
     start(has_s, near_s)
-    start(None, x_heat)
 
     loads[1].wait()
     for k in range(depth):
@@ -265,6 +255,12 @@
             here = (lane >= STEP * t - 2) & (lane < STEP * t + 2)
             acc = jnp.where(here, picked[t * ROWS : (t + 1) * ROWS], acc)
         col_ed[k] = acc
+        if k % PAIR == 0:
+            even = acc
+        else:
+            moved = pltpu.roll(acc, STEP // 2, 1)
+            send_w[k // PAIR] = jnp.where(lane % STEP < 2, even, moved)
+            send_e[k // PAIR] = jnp.where(lane % STEP < 2, moved, even)
     start(has_e, edge_e)
     start(has_w, edge_w)
     for c, send, _ in corners:
@@ -336,15 +332,13 @@
     side_b = lax.broadcasted_iota(jnp.int32, (LANES, LANES), 1) % STEP
     across = split(jnp.where((side_a == side_b) & ((side_a == 0) | (side_a == STEP - 1)), across, 0.0))
 
-    wait_recv(has_s, rows_n + depth_n)
-    wait_recv(has_n, rows_s + depth_s)
-    wait_recv(None, x_main)
+    wait_recv(has_s, rows_n[:1] + depth_n)
+    wait_recv(has_n, rows_s[:1] + depth_s)
 
     lane2 = lax.broadcasted_iota(jnp.int32, (EXT, LANES), 1)
     window = (lane2 < 2) | (lane2 >= LANES - 3)
 
-    def field(f, k):
-        q, l = k // share, k % share
+    def field(f, q, l):
         g = GROUP * (f * share + l)
         held = tall[q, 3 * share]
         moved = pltpu.roll(held, (LANES - g) % LANES, 1) if g else held
@@ -361,35 +355,42 @@
     spot = (s * ROWS + jnp.where(line < 12, line, line - EXT)).astype(F32)
     fcor = 0.3 * (2.0 * (spot + 0.5) / (nstrip * ROWS) - 1.0)
 
+    layers_u, layers_v = jnp.minimum(layers, east(layers)), jnp.minimum(layers, north(layers))
+
     def masks(k):
-        wet = (k < layers).astype(F32)
-        return wet, wet * east(wet), wet * north(wet)
+        return [(k < n).astype(F32) for n in (layers, layers_u, layers_v)]
 
     def advance(m, u, v, t):
-        new_u = m[1] * (u + 0.1 * lap(u) + fcor * v - 0.2 * (east(t) - t))
-        new_v = m[2] * (v + 0.1 * lap(v) - fcor * u - 0.2 * (north(t) - t))
+        push = 0.2 * t
+        new_u = m[1] * (0.6 * u + east(0.1 * u - push) + 0.1 * (west(u) + north(u) + south(u)) + fcor * v + push)
+        new_v = m[2] * (0.6 * v + north(0.1 * v - push) + 0.1 * (east(v) + west(v) + south(v)) - fcor * u + push)
         return new_u, new_v
 
-    for k in range(depth):
-        u1, v1 = advance(masks(k), field(0, k), field(1, k), field(2, k))
-        flow[0, k], flow[1, k] = u1, v1
-        for i, a in enumerate(upwind(u1, west(u1), v1, south(v1))):
-            cex[i, k] = a[:, 0:LANES]
-            cec[i, k] = a[0:ROWS, LANES:WIDE]
-    wait_recv(None, x_heat)
-    for k in range(depth):
-        m = masks(k)
-        t0 = field(2, k)
-        t1 = m[0] * (t0 + 0.1 * lap(t0) + 0.5 * field(3, k))
-        u2, v2 = advance(m, flow[0, k], flow[1, k], t1)
-        u_here, v_here = u2[0:ROWS, 0:LANES], v2[0:ROWS, 0:LANES]
-        u_back, v_back = west(u2)[0:ROWS, 0:LANES], south(v2)[0:ROWS, 0:LANES]
-        for i, a in enumerate(upwind(u_here, u_back, v_here, v_back)):
-            cf1[i, k] = a
-        t_base[k] = (m[0] * (t1 + 0.1 * lap(t1)))[0:ROWS, 0:LANES]
-        o_send[0, k] = u_here
-        o_send[1, k] = v_here
-    start(None, flow_out)
+    def both_steps(q):
+        for l in range(share):
+            k = q * share + l
+            m = masks(k)
+            u0, v0, t0, h0 = (field(f, q, l) for f in range(4))
+            u1, v1 = advance(m, u0, v0, t0)
+            for i, a in enumerate(upwind(u1, west(u1), v1, south(v1))):
+                cex[i, k] = a[:, 0:LANES]
+                cec[i, k] = a[0:ROWS, LANES:WIDE]
+            t1 = m[0] * (t0 + 0.1 * lap(t0) + 0.5 * h0)
+            u2, v2 = advance(m, u1, v1, t1)
+            u_here, v_here = u2[0:ROWS, 0:LANES], v2[0:ROWS, 0:LANES]
+            u_back, v_back = west(u2)[0:ROWS, 0:LANES], south(v2)[0:ROWS, 0:LANES]
+            for i, a in enumerate(upwind(u_here, u_back, v_here, v_back)):
+                cf1[i, k] = a
+            t_base[k] = (m[0] * (t1 + 0.1 * lap(t1)))[0:ROWS, 0:LANES]
+            o_send[0, k] = u_here
+            o_send[1, k] = v_here
+
+    both_steps(col)
+    for d, _ in others(1):
+        wait_recv(has_s, rows_n[d : d + 1])
+        wait_recv(has_n, rows_s[d : d + 1])
+        wait_recv(None, x_main[d - 1 : d])
+        both_steps(lax.rem(col + nlon - d, nlon))
     out[0:2, :, :, cols(col)] = o_send[0:2, mine]
 
     def coefs(m, k):
@@ -439,7 +440,10 @@
         return (k < level_main).astype(F32) * (value + (0.5 * top) * gain)
 
     def sideways(k):
-        return jnp.where(lane % STEP < 2, got_e[k], got_w[k])
+        e, w = got_e[k // PAIR], got_w[k // PAIR]
+        if k % PAIR:
+            e, w = (pltpu.roll(x, LANES - STEP // 2, 1) for x in (e, w))
+        return jnp.where(lane % STEP < 2, e, w)
 
     def ring_rows():
         tops, wets = [], []
@@ -505,6 +509,7 @@
     wait_recv(has_n, near_s)
     wait_recv(has_w, edge_e)
     wait_recv(has_e, edge_w)
+    start(None, flow_out)
     leads, firsts = [], []
     for levels in groups:
         edges = unpack(*(sideways(k) for k in levels))
@@ -557,7 +562,7 @@
         for k, block, gain in zip(levels, blocks, gains):
             c_out[:, k] = settle(k, last[k], block.reshape(tracers, ROWS, LANES), gain)
 
-    wait_send(None, x_main + x_heat)
+    wait_send(None, x_main)
     wait_send(has_n, rows_n + depth_n + near_n + far_n)
     wait_send(has_s, rows_s + depth_s + near_s + far_s)
     wait_send(has_e, edge_e)
@@ -603,7 +608,7 @@
             buf(c.shape, F32), buf(c.shape, F32), buf(c.shape, F32),
             buf((2,) + line, F32), buf((2,) + line, F32),
             buf(line, F32), buf(line, F32), buf(line, F32), buf(line, F32),
-            buf((depth,) + tile, F32), buf((depth,) + tile, F32), buf((depth,) + tile, F32),
+            buf((depth,) + tile, F32), *([buf((depth // PAIR,) + tile, F32)] * 4),
             buf((2, 2, depth, LANES), F32),
             buf((depth,) + tile, F32), buf((depth,) + tile, F32), buf((depth, LANES), F32), buf((depth, LANES), F32),
             buf((5, depth, EXT, LANES), F32),
@@ -613,7 +618,7 @@
             buf((4, depth) + tile, F32),
             buf(r.shape, F32),
             dma((3,)), dma((4, nlon)),
-            *(pair * 4),
+            *(pair * 3),
             dma((2,)), dma((2,)), dma((6,)), dma((6,)), dma((4,)), dma((4,)),
             *(pair * 3),
         ],

time: 14.6 us -> 14.2 us (0.973)
  Pallas kernels: 13.8 us -> 13.4 us
    pallas_call x1, Pallas kernels: 12.8 us -> 12.4 us  [shards(): pl.pallas_call(functools.partial(kernel, sizes), out_shape=(buf((4, share...]
where the time goes in v3:
time: 14.2 us; the launch traced here: 14 us
  Pallas kernels  13.4 us (94%)
  between operations  0.64 us (5%)
    pallas_call x1, Pallas kernels, shards(): pl.pallas_call(functools.partial(kernel, sizes), out_shape=(buf((4, share...  12.4 us
    pallas_call x1, Pallas kernels, shards(): pl.pallas_call(store, out_shape=(strip, strip, strip, strip, jax.ShapeDty...  0.95 us

profile of v3, /device:TPU:0, one launch (start us, length us, event | category | flops | bytes accessed | tf_op | source)
XLA Modules:
  0.0 14.0 jit_solution(1848057883056380661)
XLA Ops:
  0.6 12.4 %shard_map.110 = (f32[4,4,8,256]{3,2,1,0:T(8,128)S(1)}, f32[24,8,8,128]{3,2,1,0:T(8,128)S(1)}) custom-call(f32[4,8,256]{2,1,0:T(8,128)} %u_hbm.1, f32[4,8,256]{2,1,0:T(8,128)} %v_hbm.1, f32[4,8,256]{2,1,0:T(8,128)} %t_hbm.1, f32[4,8,256]{2,1,0:T(8,128)} %h_hbm.1, f32[24,8,8,128]{3,2,1,0:T(8,128)} %c_hbm.1, s32[8,256]{1,0:T(8,128)} %n_hbm.1, f32[24,24]{1,0:T(8,128)} %r_hbm.1), custom_call_target="tpu_custom_call" | custom-call | tf_op jit(solution)/shard_map/pallas_call | solution.py:598
  13.0 1.0 %shard_map.111 = (f32[4,8,256]{2,1,0:T(8,128)}, f32[4,8,256]{2,1,0:T(8,128)}, f32[4,8,256]{2,1,0:T(8,128)}, f32[4,8,256]{2,1,0:T(8,128)}, f32[24,8,8,128]{3,2,1,0:T(8,128)}) custom-call(f32[4,4,8,256]{3,2,1,0:T(8,128)S(1)} %get-tuple-element.7.out, f32[24,8,8,128]{3,2,1,0:T(8,128)S(1)} %get-tuple-element.8.c_out), custom_call_target="tpu_custom_call" | custom-call | tf_op jit(solution)/shard_map/pallas_call | solution.py:629

commit v4 on v3

--- a/solution.py
+++ b/solution.py
@@ -75,14 +75,14 @@
     sizes,
     u_hbm, v_hbm, t_hbm, h_hbm, c_hbm, n_hbm, r_hbm,
     out, c_out,
-    stage, tall, flow, cnt, c_in, c_raw, c_mid, row_n, row_s, raw_n, raw_s, ring_n, ring_s,
+    stage, tall, flow, cnt, c_in, c_east, c_west, c_raw, c_mid, row_n, row_s, raw_n, raw_s, ring_n, ring_s,
     col_ed, send_e, send_w, got_e, got_w, cor, ring_c, lead_c, lead_n, lead_s, cex, cec, cf1, t_base, o_send, r_in, in_sem, strip_sem,
     x_ss, x_rs, n_ss, n_rs, s_ss, s_rs,
     k_ss, k_rs, c_ss, c_rs, q_ss, q_rs, uv_ss, uv_rs, t_ss, t_rs, h_ss, h_rs,
 ):
     tracers, depth, share, nlon, nrole, nstrip = sizes
     def slot(f, l):
-        return f * share + l + (f == 3)
+        return (0, 2 * share, share, 3 * share + 1)[f] + l
 
     strip_loads = [
         pltpu.make_async_copy(
@@ -163,14 +163,21 @@
         copy(stage.at[p], tall.at[col, :, 0:ROWS], x_ss.at[d], x_rs.at[d], {"lon": p})
         for d, p in others(1)
     ]
-    rows_n = [
-        copy(stage.at[p, :, 5:8], tall.at[col, :, 13:16], n_ss.at[d], n_rs.at[d], dict(to_n, lon=p))
-        for d, p in others(0)
-    ]
-    rows_s = [
-        copy(stage.at[p, :, 0:2], tall.at[col, :, 8:10], s_ss.at[d], s_rs.at[d], dict(to_s, lon=p))
-        for d, p in others(0)
-    ]
+    late, last = 3 * share + 1, 4 * share + 1
+    cuts_n = ((0, 2 * share, 6, 8), (2 * share, late, 5, 8), (late, last, 7, 8))
+    cuts_s = ((0, late, 0, 2), (late, last, 0, 1))
+
+    def rows(cuts, ss, rs, dev, d, p):
+        return [
+            copy(
+                stage.at[p, a:b, lo:hi], tall.at[col, a:b, ROWS + lo : ROWS + hi],
+                ss.at[i, d], rs.at[i, d], dict(dev, lon=p),
+            )
+            for i, (a, b, lo, hi) in enumerate(cuts)
+        ]
+
+    rows_n = [rows(cuts_n if d else ((0, last, 5, 8),), n_ss, n_rs, to_n, d, p) for d, p in others(0)]
+    rows_s = [rows(cuts_s if d else ((0, last, 0, 2),), s_ss, s_rs, to_s, d, p) for d, p in others(0)]
     depth_n = [copy(n_hbm.at[6:8], cnt.at[14:16], k_ss.at[0], k_rs.at[0], to_n)]
     depth_s = [copy(n_hbm.at[0:2], cnt.at[8:10], k_ss.at[1], k_rs.at[1], to_s)]
     near_n = [copy(c_hbm.at[:, :, 7, :], row_s.at[0], c_ss.at[0], c_rs.at[0], to_n)]
@@ -239,9 +246,11 @@
         stage[p, 3 * share] = acc
 
     pl.semaphore_wait(barrier, nlon - 1 + nlon * (jnp.minimum(s, 1) + jnp.minimum(nstrip - 1 - s, 1)))
-    start(has_n, rows_n[::-1] + depth_n)
-    start(has_s, rows_s[::-1] + depth_s)
+    start(has_n, sum(rows_n[1:], []))
+    start(has_s, sum(rows_s[1:], []))
     start(None, x_main)
+    start(has_n, rows_n[0] + depth_n)
+    start(has_s, rows_s[0] + depth_s)
     start(has_n, near_n)
     start(has_s, near_s)
 
@@ -332,8 +341,13 @@
     side_b = lax.broadcasted_iota(jnp.int32, (LANES, LANES), 1) % STEP
     across = split(jnp.where((side_a == side_b) & ((side_a == 0) | (side_a == STEP - 1)), across, 0.0))
 
-    wait_recv(has_s, rows_n[:1] + depth_n)
-    wait_recv(has_n, rows_s[:1] + depth_s)
+    for k in range(depth):
+        for t in range(tracers):
+            c_east[t, k] = pltpu.roll(c_in[t, k], LANES - 1, 1)
+            c_west[t, k] = pltpu.roll(c_in[t, k], 1, 1)
+
+    wait_recv(has_s, rows_n[0] + depth_n)
+    wait_recv(has_n, rows_s[0] + depth_s)
 
     lane2 = lax.broadcasted_iota(jnp.int32, (EXT, LANES), 1)
     window = (lane2 < 2) | (lane2 >= LANES - 3)
@@ -365,6 +379,9 @@
         new_u = m[1] * (0.6 * u + east(0.1 * u - push) + 0.1 * (west(u) + north(u) + south(u)) + fcor * v + push)
         new_v = m[2] * (0.6 * v + north(0.1 * v - push) + 0.1 * (east(v) + west(v) + south(v)) - fcor * u + push)
         return new_u, new_v
+
+    def both(x):
+        return jnp.where(eastern, jnp.broadcast_to(x[:, 0:1], x.shape), jnp.broadcast_to(x[:, LANES - 1 :], x.shape))
 
     def both_steps(q):
         for l in range(share):
@@ -374,7 +391,7 @@
             u1, v1 = advance(m, u0, v0, t0)
             for i, a in enumerate(upwind(u1, west(u1), v1, south(v1))):
                 cex[i, k] = a[:, 0:LANES]
-                cec[i, k] = a[0:ROWS, LANES:WIDE]
+                cec[i, k] = both(a[0:ROWS, LANES:WIDE])
             t1 = m[0] * (t0 + 0.1 * lap(t0) + 0.5 * h0)
             u2, v2 = advance(m, u1, v1, t1)
             u_here, v_here = u2[0:ROWS, 0:LANES], v2[0:ROWS, 0:LANES]
@@ -387,8 +404,8 @@
 
     both_steps(col)
     for d, _ in others(1):
-        wait_recv(has_s, rows_n[d : d + 1])
-        wait_recv(has_n, rows_s[d : d + 1])
+        wait_recv(has_s, rows_n[d])
+        wait_recv(has_n, rows_s[d])
         wait_recv(None, x_main[d - 1 : d])
         both_steps(lax.rem(col + nlon - d, nlon))
     out[0:2, :, :, cols(col)] = o_send[0:2, mine]
@@ -398,11 +415,13 @@
             return [cex[i, k, 0:ROWS, :] for i in range(5)]
         return [cf1[i, k] for i in range(5)]
 
-    def advect(a, x, edge, above, below):
+    def advect(a, x, edge, above, below, x_e=None, x_w=None):
+        if x_e is None:
+            x_e, x_w = pltpu.roll(x, LANES - 1, 1), pltpu.roll(x, 1, 1)
         x_n = jnp.where(row == ROWS - 1, above, pltpu.roll(x, ROWS - 1, 0))
         x_s = jnp.where(row == 0, below, pltpu.roll(x, 1, 0))
-        x_e = jnp.where(lane == LANES - 1, edge, pltpu.roll(x, LANES - 1, 1))
-        x_w = jnp.where(lane == 0, edge, pltpu.roll(x, 1, 1))
+        x_e = jnp.where(lane == LANES - 1, edge, x_e)
+        x_w = jnp.where(lane == 0, edge, x_w)
         return mix(a, x, x_e, x_w, x_n, x_s)
 
     def lead_of(values):
@@ -478,11 +497,6 @@
             ring[...] = wets[i] * (blocks[i] + (0.5 * tops[i]) * gains[i])
 
     def ring_cols():
-        def both(x):
-            return jnp.where(
-                eastern, jnp.broadcast_to(x[:, 0:1], x.shape), jnp.broadcast_to(x[:, LANES - 1 :], x.shape)
-            )
-
         edge_n = jnp.where(lane % STEP < 2, cor[0, 0], cor[0, 1])
         edge_s = jnp.where(lane % STEP < 2, cor[1, 0], cor[1, 1])
         wet_n = both(n_side[0:ROWS])
@@ -490,7 +504,7 @@
         values, tops = [], []
         for k in range(depth):
             x, own = sideways(k), col_ed[k]
-            a = [both(cec[i, k]) for i in range(5)]
+            a = [cec[i, k] for i in range(5)]
             x_e = pltpu.roll(jnp.where(eastern, own, x), LANES - 1, 1)
             x_w = pltpu.roll(jnp.where(western, own, x), 1, 1)
             x_n = jnp.where(row == ROWS - 1, edge_n[k : k + 1, :], pltpu.roll(x, ROWS - 1, 0))
@@ -516,7 +530,10 @@
         for i, k in enumerate(levels):
             a = coefs(0, k)
             values = [
-                advect(a, c_in[t, k], edges[t][i], row_n[0, t, k : k + 1, :], row_s[0, t, k : k + 1, :])
+                advect(
+                    a, c_in[t, k], edges[t][i], row_n[0, t, k : k + 1, :], row_s[0, t, k : k + 1, :],
+                    c_east[t, k], c_west[t, k],
+                )
                 for t in range(tracers)
             ]
             for t in range(tracers):
@@ -563,8 +580,8 @@
             c_out[:, k] = settle(k, last[k], block.reshape(tracers, ROWS, LANES), gain)
 
     wait_send(None, x_main)
-    wait_send(has_n, rows_n + depth_n + near_n + far_n)
-    wait_send(has_s, rows_s + depth_s + near_s + far_s)
+    wait_send(has_n, sum(rows_n, []) + depth_n + near_n + far_n)
+    wait_send(has_s, sum(rows_s, []) + depth_s + near_s + far_s)
     wait_send(has_e, edge_e)
     wait_send(has_w, edge_w)
     for c, send, _ in corners:
@@ -605,7 +622,7 @@
             buf((nlon, 4 * share + 1, EXT, LANES), F32),
             buf((2, depth, EXT, WIDE), F32),
             buf((EXT, width), jnp.int32),
-            buf(c.shape, F32), buf(c.shape, F32), buf(c.shape, F32),
+            *([buf(c.shape, F32)] * 5),
             buf((2,) + line, F32), buf((2,) + line, F32),
             buf(line, F32), buf(line, F32), buf(line, F32), buf(line, F32),
             buf((depth,) + tile, F32), *([buf((depth // PAIR,) + tile, F32)] * 4),
@@ -618,7 +635,7 @@
             buf((4, depth) + tile, F32),
             buf(r.shape, F32),
             dma((3,)), dma((4, nlon)),
-            *(pair * 3),
+            *pair, dma((3, nlon)), dma((3, nlon)), dma((2, nlon)), dma((2, nlon)),
             dma((2,)), dma((2,)), dma((6,)), dma((6,)), dma((4,)), dma((4,)),
             *(pair * 3),
         ],

time: 14.2 us -> 14 us (0.986)
  Pallas kernels: 13.4 us -> 13.2 us
where the time goes in v4:
time: 14 us; the launch traced here: 13.9 us
  Pallas kernels  13.2 us (94%)
  between operations  0.64 us (5%)
    pallas_call x1, Pallas kernels, shards(): pl.pallas_call(functools.partial(kernel, sizes), out_shape=(buf((4, share...  12.3 us
    pallas_call x1, Pallas kernels, shards(): pl.pallas_call(store, out_shape=(strip, strip, strip, strip, jax.ShapeDty...  0.95 us

profile of v4, /device:TPU:0, one launch (start us, length us, event | category | flops | bytes accessed | tf_op | source)
XLA Modules:
  0.0 13.9 jit_solution(16585726783763131060)
XLA Ops:
  0.6 12.3 %shard_map.110 = (f32[4,4,8,256]{3,2,1,0:T(8,128)S(1)}, f32[24,8,8,128]{3,2,1,0:T(8,128)S(1)}) custom-call(f32[4,8,256]{2,1,0:T(8,128)} %u_hbm.1, f32[4,8,256]{2,1,0:T(8,128)} %v_hbm.1, f32[4,8,256]{2,1,0:T(8,128)} %t_hbm.1, f32[4,8,256]{2,1,0:T(8,128)} %h_hbm.1, f32[24,8,8,128]{3,2,1,0:T(8,128)} %c_hbm.1, s32[8,256]{1,0:T(8,128)} %n_hbm.1, f32[24,24]{1,0:T(8,128)} %r_hbm.1), custom_call_target="tpu_custom_call" | custom-call | tf_op jit(solution)/shard_map/pallas_call | solution.py:615
  12.9 1.0 %shard_map.111 = (f32[4,8,256]{2,1,0:T(8,128)}, f32[4,8,256]{2,1,0:T(8,128)}, f32[4,8,256]{2,1,0:T(8,128)}, f32[4,8,256]{2,1,0:T(8,128)}, f32[24,8,8,128]{3,2,1,0:T(8,128)}) custom-call(f32[4,4,8,256]{3,2,1,0:T(8,128)S(1)} %get-tuple-element.7.out, f32[24,8,8,128]{3,2,1,0:T(8,128)S(1)} %get-tuple-element.8.c_out), custom_call_target="tpu_custom_call" | custom-call | tf_op jit(solution)/shard_map/pallas_call | solution.py:646

commit v5 on v4

--- a/solution.py
+++ b/solution.py
@@ -251,8 +251,6 @@
     start(None, x_main)
     start(has_n, rows_n[0] + depth_n)
     start(has_s, rows_s[0] + depth_s)
-    start(has_n, near_n)
-    start(has_s, near_s)
 
     loads[1].wait()
     for k in range(depth):
@@ -272,6 +270,8 @@
             send_e[k // PAIR] = jnp.where(lane % STEP < 2, moved, even)
     start(has_e, edge_e)
     start(has_w, edge_w)
+    start(has_n, near_n)
+    start(has_s, near_s)
     for c, send, _ in corners:
         start(send, [c])
     start(has_n, far_n)
@@ -408,6 +408,7 @@
         wait_recv(has_n, rows_s[d])
         wait_recv(None, x_main[d - 1 : d])
         both_steps(lax.rem(col + nlon - d, nlon))
+    start(None, flow_out)
     out[0:2, :, :, cols(col)] = o_send[0:2, mine]
 
     def coefs(m, k):
@@ -523,7 +524,6 @@
     wait_recv(has_n, near_s)
     wait_recv(has_w, edge_e)
     wait_recv(has_e, edge_w)
-    start(None, flow_out)
     leads, firsts = [], []
     for levels in groups:
         edges = unpack(*(sideways(k) for k in levels))

time: 14 us -> 14.1 us (level)
  no operation moved by 1% of the time
where the time goes in v5:
time: 14.1 us; the launch traced here: 13.9 us
  Pallas kernels  13.3 us (94%)
  between operations  0.64 us (5%)
    pallas_call x1, Pallas kernels, shards(): pl.pallas_call(functools.partial(kernel, sizes), out_shape=(buf((4, share...  12.3 us
    pallas_call x1, Pallas kernels, shards(): pl.pallas_call(store, out_shape=(strip, strip, strip, strip, jax.ShapeDty...  0.95 us

profile of v5, /device:TPU:0, one launch (start us, length us, event | category | flops | bytes accessed | tf_op | source)
XLA Modules:
  0.0 13.9 jit_solution(16152414651168289209)
XLA Ops:
  0.6 12.3 %shard_map.110 = (f32[4,4,8,256]{3,2,1,0:T(8,128)S(1)}, f32[24,8,8,128]{3,2,1,0:T(8,128)S(1)}) custom-call(f32[4,8,256]{2,1,0:T(8,128)} %u_hbm.1, f32[4,8,256]{2,1,0:T(8,128)} %v_hbm.1, f32[4,8,256]{2,1,0:T(8,128)} %t_hbm.1, f32[4,8,256]{2,1,0:T(8,128)} %h_hbm.1, f32[24,8,8,128]{3,2,1,0:T(8,128)} %c_hbm.1, s32[8,256]{1,0:T(8,128)} %n_hbm.1, f32[24,24]{1,0:T(8,128)} %r_hbm.1), custom_call_target="tpu_custom_call" | custom-call | tf_op jit(solution)/shard_map/pallas_call | solution.py:615
  12.9 1.0 %shard_map.111 = (f32[4,8,256]{2,1,0:T(8,128)}, f32[4,8,256]{2,1,0:T(8,128)}, f32[4,8,256]{2,1,0:T(8,128)}, f32[4,8,256]{2,1,0:T(8,128)}, f32[24,8,8,128]{3,2,1,0:T(8,128)}) custom-call(f32[4,4,8,256]{3,2,1,0:T(8,128)S(1)} %get-tuple-element.7.out, f32[24,8,8,128]{3,2,1,0:T(8,128)S(1)} %get-tuple-element.8.c_out), custom_call_target="tpu_custom_call" | custom-call | tf_op jit(solution)/shard_map/pallas_call | solution.py:646
